TPU v7x, 128 devices: a whole 4x4x4 slice. The times are simulated.
128 devices in a mesh: wide: 32 (over y, x, core), cross: 4 (over z).
Axes of the slice: x: 4, y: 4, z: 4, core: 2. Of those that a mesh axis runs over, the one named last changes fastest.
Arguments:
- rhs: float32 [3, 128, 32, 257], P(None, 'wide', 'cross'), may hold values from -6 to 6
- start: float32 [3, 128, 32, 257], P(None, 'wide', 'cross'), may hold values from -6 to 6
- stiffness: float32 [32, 8, 64], P('wide', 'cross'), may hold values from 1 to 10
- fibre_index: int32 [32, 8, 64], P('wide', 'cross'), may hold values from 0 to 63
Outputs:
- solution: float32 [3, 128, 32, 257], P(None, 'wide', 'cross')
- correction: float32 [3, 32, 8, 65], P(None, 'wide', 'cross')
All inputs are finite; a program needn't handle non-finite values.
Results may differ from a plain program's by a relative error of at most 0.0003.
Values sent between devices are 32-bit elements; how exact they have to be, the bound alone decides.
A program may use at most 128 MiB of HBM per device.

v0:
```python
import math

import jax
import jax.numpy as jnp
import numpy as np
from jax import lax
from jax.sharding import PartitionSpec as P

NFIB = 64


LAMBDA_COEF = 2.0
SHEAR_CROSS = 1.0
SHEAR_ALONG = 3.0
FIBRE_COEF = 20.0
MASS_COEF = 0.02
FINE_RATIO = 10.0
COARSE_RATIO = 30.0


def passed_along(block, axis, distance):
    devices = range(lax.axis_size(axis))
    route = [(i - distance, i) for i in devices if i - distance in devices]
    return lax.ppermute(block, axis, route)


def gll_points():
    root = math.sqrt(3.0 / 7.0)
    points = (np.array([-1.0, -root, 0.0, root, 1.0]) + 1.0) / 2.0
    weights = np.array([0.1, 49.0 / 90.0, 32.0 / 45.0, 49.0 / 90.0, 0.1]) / 2.0
    return (points, weights)


def lagrange_slopes(points, where):
    count = len(points)
    table = np.zeros((len(where), count))
    for i, spot in enumerate(where):
        for j in range(count):
            total = 0.0
            for k in range(count):
                if k == j:
                    continue
                term = 1.0 / (points[j] - points[k])
                for m in range(count):
                    if m != j and m != k:
                        term = term * (spot - points[m]) / (points[j] - points[m])
                total = total + term
            table[i, j] = total
    return table


def element_tables(degree):
    if degree == 4:
        points, weights = gll_points()
        basis = np.eye(5)
        slopes = lagrange_slopes(points, points)
    else:
        gauss = np.array([0.5 - 0.5 / math.sqrt(3.0), 0.5 + 0.5 / math.sqrt(3.0)])
        basis = np.stack([1.0 - gauss, gauss], 1)
        slopes = np.array([[-1.0, 1.0], [-1.0, 1.0]])
        weights = np.array([0.5, 0.5])
    cube = weights[:, None, None] * weights[None, :, None] * weights[None, None, :]
    return (
        jnp.asarray(basis, dtype=jnp.float32),
        jnp.asarray(slopes, dtype=jnp.float32),
        jnp.asarray(cube, dtype=jnp.float32),
    )


def prolong_table(count, rows):
    points, weights = gll_points()
    table = np.zeros((rows, count + 1))
    for r in range(rows):
        elem, i = divmod(r, 4)
        if elem == count:
            table[r, count] = 1.0
        else:
            table[r, elem] = 1.0 - points[i]
            table[r, elem + 1] = points[i]
    return jnp.asarray(table, dtype=jnp.float32)


def fibre_vectors(index):
    angle = index.astype(jnp.float32) * (2.0 * math.pi / NFIB)
    tilt = 0.4 * jnp.sin(3.0 * angle)
    return jnp.stack(
        [jnp.cos(angle) * jnp.cos(tilt), jnp.sin(angle) * jnp.cos(tilt), jnp.sin(tilt)]
    )


def contract(field, table, axis):
    forms = ("qa,abce->qbce", "qb,abce->aqce", "qc,abce->abqe")
    return jnp.einsum(forms[axis], table, field, precision=lax.Precision.HIGHEST)


def element_apply(local, basis, slopes, cube, stiff, fibre, plain):
    gradient = [[None] * 3 for _ in range(3)]
    values = []
    for c in range(3):
        for d in range(3):
            if plain:
                gradient[c][d] = contract(local[c], slopes, d)
            else:
                field = local[c]
                for a in range(3):
                    field = contract(field, slopes if a == d else basis, a)
                gradient[c][d] = field
        if plain:
            values.append(local[c])
        else:
            field = local[c]
            for a in range(3):
                field = contract(field, basis, a)
            values.append(field)
    strain = [[0.5 * (gradient[i][j] + gradient[j][i]) for j in range(3)] for i in range(3)]
    trace_sum = strain[0][0] + strain[1][1] + strain[2][2]
    along = [
        strain[i][0] * fibre[0] + strain[i][1] * fibre[1] + strain[i][2] * fibre[2]
        for i in range(3)
    ]
    stretch = fibre[0] * along[0] + fibre[1] * along[1] + fibre[2] * along[2]
    weighted = cube[..., None] * stiff
    mass_weight = MASS_COEF * cube[..., None]
    result = []
    for c in range(3):
        field = values[c] * mass_weight
        if not plain:
            for a in range(3):
                field = contract(field, basis.T, a)
        total = field
        for d in range(3):
            stress = 2.0 * SHEAR_CROSS * strain[c][d]
            stress = stress + 2.0 * (SHEAR_ALONG - SHEAR_CROSS) * (
                fibre[c] * along[d] + along[c] * fibre[d]
            )
            stress = stress + FIBRE_COEF * stretch * fibre[c] * fibre[d]
            if c == d:
                stress = stress + LAMBDA_COEF * trace_sum
            field = stress * weighted
            if plain:
                field = contract(field, slopes.T, d)
            else:
                for a in range(3):
                    field = contract(field, (slopes if a == d else basis).T, a)
            total = total + field
        result.append(total)
    return jnp.stack(result)


def to_local(field, degree):
    count = (field.shape[-1] - 1) // degree
    first = field[..., :-1].reshape(field.shape[:-1] + (count, degree))
    last = field[..., degree::degree]
    return jnp.concatenate([first, last[..., None]], -1)


def from_local(field, degree):
    count = field.shape[-2]
    lead = field.shape[:-2]
    main = field[..., :degree].reshape(lead + (count * degree,))
    tail = jnp.concatenate(
        [jnp.zeros(lead + (count, degree - 1), field.dtype), field[..., degree:]], -1
    )
    tail = tail.reshape(lead + (count * degree,))
    spare = [(0, 0)] * len(lead)
    return jnp.pad(main, spare + [(0, 1)]) + jnp.pad(tail, spare + [(1, 0)])


def apply_operator(extended, degree, stiff, fibre):
    basis, slopes, cube = element_tables(degree)
    nodes = degree + 1
    view = to_local(extended, degree)
    view = to_local(jnp.moveaxis(view, 2, -1), degree)
    view = to_local(jnp.moveaxis(view, 1, -1), degree)
    counts = (view.shape[5], view.shape[3], view.shape[1])
    view = jnp.transpose(view, (0, 6, 4, 2, 5, 3, 1)).reshape(3, nodes, nodes, nodes, -1)
    result = element_apply(view, basis, slopes, cube, stiff, fibre, degree == 4)
    result = result.reshape((3, nodes, nodes, nodes) + counts)
    result = jnp.transpose(result, (0, 6, 3, 5, 2, 4, 1))
    result = jnp.moveaxis(from_local(result, degree), -1, 1)
    result = jnp.moveaxis(from_local(result, degree), -1, 2)
    return from_local(result, degree)


def fine_apply(field, stiff, fibre):
    after = passed_along(field[:, :1], "wide", -1)
    extended = jnp.concatenate([field, after], 1)
    beside = passed_along(extended[:, :, :1], "cross", -1)
    extended = jnp.concatenate([extended, beside], 2)
    result = apply_operator(extended, 4, stiff, fibre)
    returned = passed_along(result[:, :, -1:], "cross", 1)
    result = jnp.concatenate([result[:, :, :1] + returned, result[:, :, 1:-1]], 2)
    returned = passed_along(result[:, -1:], "wide", 1)
    return jnp.concatenate([result[:, :1] + returned, result[:, 1:-1]], 1)


def coarse_apply(field, stiff, fibre):
    after = passed_along(field, "wide", -1)
    extended = jnp.concatenate([field, after], 1)
    beside = passed_along(extended[:, :, :1], "cross", -1)
    extended = jnp.concatenate([extended, beside], 2)
    result = apply_operator(extended, 1, stiff, fibre)
    returned = passed_along(result[:, :, -1:], "cross", 1)
    result = jnp.concatenate([result[:, :, :1] + returned, result[:, :, 1:-1]], 2)
    returned = passed_along(result[:, -1:], "wide", 1)
    result = jnp.concatenate([result[:, :1] + returned, result[:, 1:-1]], 1)
    return result


def coarse_total(field):
    return lax.psum(jnp.sum(field * field), ("wide", "cross"))


def fine_total(field):
    return lax.psum(jnp.sum(field * field), ("wide", "cross"))


def apply_axis(field, table, axis):
    forms = ("ra,cabd->crbd", "rb,cabd->card", "rd,cabd->cabr")
    return jnp.einsum(forms[axis], table, field, precision=lax.Precision.HIGHEST)


def power_estimate(start_vec, operator, total):
    vector = start_vec / jnp.sqrt(total(start_vec) + 1e-06)
    square = None
    for k in range(3):
        image = operator(vector)
        square = total(image)
        vector = image / jnp.sqrt(square + 1e-06)
    return jnp.sqrt(square + 1e-06)


def chebyshev(approx, residual, largest, ratio_value, operator, keep):
    upper = 1.1 * largest
    lower = upper / ratio_value
    centre = 0.5 * (upper + lower)
    radius = 0.5 * (upper - lower)
    spread_ratio = centre / radius
    weight_old = 1.0 / spread_ratio
    step = residual / centre
    for k in range(4):
        approx = approx + step
        if k < 3 or keep:
            residual = residual - operator(step)
        if k < 3:
            weight_new = 1.0 / (2.0 * spread_ratio - weight_old)
            step = weight_new * weight_old * step + 2.0 * weight_new / radius * residual
            weight_old = weight_new
    return (approx, residual)


def on_device(rhs, start, stiffness, fibre_index):
    count_x, count_y, count_z = stiffness.shape
    stiff = stiffness.reshape(-1)
    fibre_grid = fibre_vectors(fibre_index)
    fibre = fibre_grid.reshape(3, -1)

    def fine_op(field):
        return fine_apply(field, stiff, fibre)

    table_x = prolong_table(count_x, 4 * count_x)
    table_y = prolong_table(count_y, 4 * count_y)
    table_z = prolong_table(count_z, 4 * count_z + 1)
    residual = rhs - fine_op(start)
    largest = power_estimate(residual, fine_op, fine_total)
    approx, residual = chebyshev(start, residual, largest, FINE_RATIO, fine_op, True)
    coarse_rhs = apply_axis(apply_axis(residual, table_z.T, 2), table_y.T, 1)
    returned = passed_along(coarse_rhs[:, :, -1:], "cross", 1)
    coarse_rhs = jnp.concatenate([coarse_rhs[:, :, :1] + returned, coarse_rhs[:, :, 1:-1]], 2)
    coarse_rhs = apply_axis(coarse_rhs, table_x.T, 0)
    returned = passed_along(coarse_rhs[:, -1:], "wide", 1)
    coarse_rhs = jnp.concatenate([coarse_rhs[:, :1] + returned, coarse_rhs[:, 1:-1]], 1)

    def coarse_op(field):
        return coarse_apply(field, stiff, fibre)

    coarse_largest = power_estimate(coarse_rhs, coarse_op, coarse_total)
    solved_rows, unused = chebyshev(
        jnp.zeros_like(coarse_rhs), coarse_rhs, coarse_largest, COARSE_RATIO, coarse_op, False
    )
    after = passed_along(solved_rows, "wide", -1)
    extended = jnp.concatenate([solved_rows, after], 1)
    beside = passed_along(extended[:, :, :1], "cross", -1)
    extended = jnp.concatenate([extended, beside], 2)
    approx = approx + apply_axis(
        apply_axis(apply_axis(extended, table_x, 0), table_y, 1), table_z, 2
    )
    residual = rhs - fine_op(approx)
    approx, unused = chebyshev(approx, residual, largest, FINE_RATIO, fine_op, False)
    return (approx, solved_rows)


def solution(mesh):
    in_specs = (
        P(None, "wide", "cross", None),
        P(None, "wide", "cross", None),
        P("wide", "cross", None),
        P("wide", "cross", None),
    )
    out_specs = (P(None, "wide", "cross", None), P(None, "wide", "cross", None))
    return jax.shard_map(
        on_device, mesh=mesh, in_specs=in_specs, out_specs=out_specs, check_vma=False
    )
```

profile of v0, /device:TPU:7, one launch (start us, length us, event | category | flops | bytes accessed | tf_op | source)
XLA Modules:
  0.0 1653.9 jit_solution(13220325592654174263)
XLA Ops:
  15.6 3.6 pad_maximum_fusion
  24.5 4.4 maximum_bitcast_fusion
  29.0 25.7 %slice.890 = f32[3,5,64,5,2]{4,3,2,1,0:T(8,128)} slice(f32[3,5,64,5,9]{4,3,2,1,0:T(8,128)} %maximum_bitcast_fusion), slice={[0:3:1], [0:5:1], [0:64:1], [0:5:1], [4:9:4]} | slice | bytes 76800 | tf_op jit(solution)/shard_map/slice | solution.py:153
  77.0 5.3 collective-permute-start.3
  83.5 67.0 %psum.56 = f32[]{:T(128)} all-reduce(f32[]{:T(128)} %get-tuple-element.128), channel_id=1, replica_groups=mesh['wide'=32,'cross'=4] {'wide','cross'}, use_global_device_ids=true, to_apply=%region_1.2 | all-reduce | flops 1 | bytes 8 | tf_op jit(solution)/shard_map/psum | solution.py:215
  154.0 4.6 collective-permute-done.4
  168.9 25.7 %slice.913 = f32[3,5,64,5,2]{4,3,2,1,0:T(8,128)} slice(f32[3,5,64,5,9]{4,3,2,1,0:T(8,128)} %maximum_bitcast_fusion.1), slice={[0:3:1], [0:5:1], [0:64:1], [0:5:1], [4:9:4]} | slice | bytes 76800 | tf_op jit(solution)/shard_map/slice | solution.py:153
  216.6 3.7 collective-permute-start.7
  222.0 65.6 %psum.57 = f32[]{:T(128)} all-reduce(f32[]{:T(128)} %multiply_reduce_fusion.1), channel_id=1, replica_groups=mesh['wide'=32,'cross'=4] {'wide','cross'}, use_global_device_ids=true, to_apply=%region_3.4 | all-reduce | flops 1 | bytes 8 | tf_op jit(solution)/shard_map/psum | solution.py:215
  291.2 4.5 collective-permute-done.8
  311.3 4.4 maximum_bitcast_fusion.2
  315.8 25.7 %slice.936 = f32[3,5,64,5,2]{4,3,2,1,0:T(8,128)} slice(f32[3,5,64,5,9]{4,3,2,1,0:T(8,128)} %maximum_bitcast_fusion.2), slice={[0:3:1], [0:5:1], [0:64:1], [0:5:1], [4:9:4]} | slice | bytes 76800 | tf_op jit(solution)/shard_map/slice | solution.py:153
  363.3 3.8 collective-permute-start.11
  368.9 65.7 %psum.58 = f32[]{:T(128)} all-reduce(f32[]{:T(128)} %multiply_reduce_fusion), channel_id=1, replica_groups=mesh['wide'=32,'cross'=4] {'wide','cross'}, use_global_device_ids=true, to_apply=%region_5.6 | all-reduce | flops 1 | bytes 8 | tf_op jit(solution)/shard_map/psum | solution.py:215
  438.2 4.5 collective-permute-done.12
  458.3 4.4 maximum_bitcast_fusion.3
  462.7 25.7 %slice.959 = f32[3,5,64,5,2]{4,3,2,1,0:T(8,128)} slice(f32[3,5,64,5,9]{4,3,2,1,0:T(8,128)} %maximum_bitcast_fusion.3), slice={[0:3:1], [0:5:1], [0:64:1], [0:5:1], [4:9:4]} | slice | bytes 76800 | tf_op jit(solution)/shard_map/slice | solution.py:153
  510.2 3.9 collective-permute-start.15
  515.9 65.4 %psum.59 = f32[]{:T(128)} all-reduce(f32[]{:T(128)} %fusion.182), channel_id=1, replica_groups=mesh['wide'=32,'cross'=4] {'wide','cross'}, use_global_device_ids=true, to_apply=%region_7.8 | all-reduce | flops 1 | bytes 8 | tf_op jit(solution)/shard_map/psum | solution.py:215
  584.9 4.5 collective-permute-done.16
  599.7 25.7 %slice.982 = f32[3,5,64,5,2]{4,3,2,1,0:T(8,128)} slice(f32[3,5,64,5,9]{4,3,2,1,0:T(8,128)} %maximum_bitcast_fusion.4), slice={[0:3:1], [0:5:1], [0:64:1], [0:5:1], [4:9:4]} | slice | bytes 76800 | tf_op jit(solution)/shard_map/slice | solution.py:153
  647.2 3.9 collective-permute-start.19
  654.2 6.0 collective-permute-done.20
  671.1 25.7 %slice.1005 = f32[3,5,64,5,2]{4,3,2,1,0:T(8,128)} slice(f32[3,5,64,5,9]{4,3,2,1,0:T(8,128)} %maximum_bitcast_fusion.5), slice={[0:3:1], [0:5:1], [0:64:1], [0:5:1], [4:9:4]} | slice | bytes 76800 | tf_op jit(solution)/shard_map/slice | solution.py:153
  720.1 3.9 collective-permute-start.23
  727.7 6.0 collective-permute-done.24
  744.6 25.7 %slice.1028 = f32[3,5,64,5,2]{4,3,2,1,0:T(8,128)} slice(f32[3,5,64,5,9]{4,3,2,1,0:T(8,128)} %maximum_bitcast_fusion.6), slice={[0:3:1], [0:5:1], [0:64:1], [0:5:1], [4:9:4]} | slice | bytes 76800 | tf_op jit(solution)/shard_map/slice | solution.py:153
  793.9 3.9 collective-permute-start.27
  801.6 6.0 collective-permute-done.28
  809.1 3.7 collective-permute-done.29
  820.0 25.7 %slice.1051 = f32[3,5,64,5,2]{4,3,2,1,0:T(8,128)} slice(f32[3,5,64,5,9]{4,3,2,1,0:T(8,128)} %maximum_bitcast_fusion.7), slice={[0:3:1], [0:5:1], [0:64:1], [0:5:1], [4:9:4]} | slice | bytes 76800 | tf_op jit(solution)/shard_map/slice | solution.py:153
  869.6 3.9 collective-permute-start.31
  875.1 3.9 collective-permute-start.32
  880.0 7.2 collective-permute-start.33
  888.5 65.4 %psum.60 = f32[]{:T(128)} all-reduce(f32[]{:T(128)} %get-tuple-element.80), channel_id=1, replica_groups=mesh['wide'=32,'cross'=4] {'wide','cross'}, use_global_device_ids=true, to_apply=%region_9.10 | all-reduce | flops 1 | bytes 8 | tf_op jit(solution)/shard_map/psum | solution.py:211
  957.4 4.2 collective-permute-done.34
  981.4 3.9 collective-permute-start.37
  986.7 65.1 %psum.61 = f32[]{:T(128)} all-reduce(f32[]{:T(128)} %get-tuple-element.73), channel_id=1, replica_groups=mesh['wide'=32,'cross'=4] {'wide','cross'}, use_global_device_ids=true, to_apply=%region_11.12 | all-reduce | flops 1 | bytes 8 | tf_op jit(solution)/shard_map/psum | solution.py:211
  1055.4 4.2 collective-permute-done.38
  1079.3 4.0 collective-permute-start.41
  1084.6 65.1 %psum.62 = f32[]{:T(128)} all-reduce(f32[]{:T(128)} %get-tuple-element.66), channel_id=1, replica_groups=mesh['wide'=32,'cross'=4] {'wide','cross'}, use_global_device_ids=true, to_apply=%region_13.14 | all-reduce | flops 1 | bytes 8 | tf_op jit(solution)/shard_map/psum | solution.py:211
  1153.3 4.2 collective-permute-done.42
  1177.5 4.0 collective-permute-start.45
  1182.8 64.9 %psum.63 = f32[]{:T(128)} all-reduce(f32[]{:T(128)} %fusion.1444), channel_id=1, replica_groups=mesh['wide'=32,'cross'=4] {'wide','cross'}, use_global_device_ids=true, to_apply=%region_15.16 | all-reduce | flops 1 | bytes 8 | tf_op jit(solution)/shard_map/psum | solution.py:211
  1251.2 4.2 collective-permute-done.46
  1275.5 3.9 collective-permute-start.49
  1282.1 5.6 collective-permute-done.50
  1309.5 3.9 collective-permute-start.53
  1316.1 5.6 collective-permute-done.54
  1343.5 3.9 collective-permute-start.57
  1350.1 5.6 collective-permute-done.58
  1363.3 5.5 collective-permute-done.60
  1379.1 25.7 %slice.1206 = f32[3,5,64,5,2]{4,3,2,1,0:T(8,128)} slice(f32[3,5,64,5,9]{4,3,2,1,0:T(8,128)} %maximum_bitcast_fusion.8), slice={[0:3:1], [0:5:1], [0:64:1], [0:5:1], [4:9:4]} | slice | bytes 76800 | tf_op jit(solution)/shard_map/slice | solution.py:153
  1428.4 3.9 collective-permute-start.63
  1435.4 6.0 collective-permute-done.64
  1452.3 25.7 %slice.1229 = f32[3,5,64,5,2]{4,3,2,1,0:T(8,128)} slice(f32[3,5,64,5,9]{4,3,2,1,0:T(8,128)} %maximum_bitcast_fusion.9), slice={[0:3:1], [0:5:1], [0:64:1], [0:5:1], [4:9:4]} | slice | bytes 76800 | tf_op jit(solution)/shard_map/slice | solution.py:153
  1500.9 3.9 collective-permute-start.67
  1508.5 6.0 collective-permute-done.68
  1525.4 25.7 %slice.1252 = f32[3,5,64,5,2]{4,3,2,1,0:T(8,128)} slice(f32[3,5,64,5,9]{4,3,2,1,0:T(8,128)} %maximum_bitcast_fusion.10), slice={[0:3:1], [0:5:1], [0:64:1], [0:5:1], [4:9:4]} | slice | bytes 76800 | tf_op jit(solution)/shard_map/slice | solution.py:153
  1574.0 3.9 collective-permute-start.71
  1581.0 6.0 collective-permute-done.72
  1588.5 3.7 collective-permute-done.73
  1599.4 25.7 %slice.1275 = f32[3,5,64,5,2]{4,3,2,1,0:T(8,128)} slice(f32[3,5,64,5,9]{4,3,2,1,0:T(8,128)} %maximum_bitcast_fusion.11), slice={[0:3:1], [0:5:1], [0:64:1], [0:5:1], [4:9:4]} | slice | bytes 76800 | tf_op jit(solution)/shard_map/slice | solution.py:153
  1648.0 3.9 collective-permute-start.75
  (1557 shorter events, 607.0 us)
Async XLA Ops:
  1.4 7.4 collective-permute-start
  8.8 4.7 collective-permute-start.1
  72.4 4.5 collective-permute-start.2
  77.0 5.9 collective-permute-start.3
  151.2 7.4 collective-permute-start.4
  158.6 4.6 collective-permute-start.5
  216.6 4.8 collective-permute-start.7
  288.4 7.4 collective-permute-start.8
  295.8 4.6 collective-permute-start.9
  363.3 4.9 collective-permute-start.11
  435.3 7.4 collective-permute-start.12
  442.7 4.6 collective-permute-start.13
  510.2 5.0 collective-permute-start.15
  582.0 7.4 collective-permute-start.16
  589.4 4.6 collective-permute-start.17
  647.2 5.0 collective-permute-start.19
  652.3 8.0 collective-permute-start.20
  660.3 5.1 collective-permute-start.21
  715.6 4.3 collective-permute-start.22
  720.1 5.0 collective-permute-start.23
  725.8 8.0 collective-permute-start.24
  733.8 5.1 collective-permute-start.25
  789.5 4.3 collective-permute-start.26
  793.9 5.0 collective-permute-start.27
  799.6 8.0 collective-permute-start.28
  807.6 5.1 collective-permute-start.29
  865.0 4.4 collective-permute-start.30
  869.6 5.0 collective-permute-start.31
  875.1 4.7 collective-permute-start.32
  880.0 7.9 collective-permute-start.33
  954.6 7.0 collective-permute-start.34
  961.6 4.3 collective-permute-start.35
  981.4 4.7 collective-permute-start.37
  1052.6 7.0 collective-permute-start.38
  1059.6 4.3 collective-permute-start.39
  1079.3 4.7 collective-permute-start.41
  1150.5 7.0 collective-permute-start.42
  1157.5 4.3 collective-permute-start.43
  1177.5 4.7 collective-permute-start.45
  1248.4 7.0 collective-permute-start.46
  1255.4 4.3 collective-permute-start.47
  1275.5 4.7 collective-permute-start.49
  1280.2 7.6 collective-permute-start.50
  1287.7 4.9 collective-permute-start.51
  1309.5 4.7 collective-permute-start.53
  1314.2 7.6 collective-permute-start.54
  1321.7 4.9 collective-permute-start.55
  1343.5 4.7 collective-permute-start.57
  1348.2 7.6 collective-permute-start.58
  1355.8 4.9 collective-permute-start.59
  1361.4 7.4 collective-permute-start.60
  1368.8 4.6 collective-permute-start.61
  1424.0 4.3 collective-permute-start.62
  1428.4 5.0 collective-permute-start.63
  1433.5 8.0 collective-permute-start.64
  1441.5 5.1 collective-permute-start.65
  1500.9 5.0 collective-permute-start.67
  1506.6 8.0 collective-permute-start.68
  1514.6 5.1 collective-permute-start.69
  1574.0 5.0 collective-permute-start.71
  1579.0 8.0 collective-permute-start.72
  1587.0 5.1 collective-permute-start.73
  1643.6 4.3 collective-permute-start.74
  1648.0 5.0 collective-permute-start.75
  (51 other events, 588.3 us)
where the time goes:
time: 1690 us; the launch traced here: 1650 us
  blocking collectives  524 us (31%)
  local copies, waits for them, and re-layouts  512 us (30%)
  starting transfers between devices  204 us (12%)
  waiting for transfers between devices  188 us (11%)
  matrix products  131 us (8%)
  other arithmetic  80.7 us (5%)
    slice x24, local copies, waits for them, and re-layouts, to_local(): last = field[..., degree::degree]  332 us
    psum x4, blocking collectives, fine_total(): return lax.psum(jnp.sum(field * field), ('wide', 'cross'))  264 us
    psum x4, blocking collectives, coarse_total(): return lax.psum(jnp.sum(field * field), ('wide', 'cross'))  261 us
    ppermute x76, starting transfers between devices, passed_along(): return lax.ppermute(block, axis, route)  204 us
    ppermute x76, waiting for transfers between devices, passed_along(): return lax.ppermute(block, axis, route)  188 us
    dot_general x594, matrix products, contract(): jnp.einsum(forms[axis], table, field, precision=lax.Precision.HIGHEST)  129 us
    transpose x18, other arithmetic, apply_operator(): view = to_local(jnp.moveaxis(view, 2, -1), degree)  39.4 us
    slice x34, local copies, waits for them, and re-layouts, to_local(): first = field[..., :-1].reshape(field.shape[:-1] + (count, degree))  39.1 us
  transfers between devices with their start and end apart: 76, of which 76 were waited for; matrix products, arithmetic and copies ran while one was open for 0% of the time, Pallas kernels for 0%

commit v1 on v0

v1 whole, which is shorter than its diff:
```python
import functools
import math

import jax
import jax.numpy as jnp
import numpy as np
from jax import lax
from jax.experimental import pallas as pl
from jax.experimental.pallas import tpu as pltpu
from jax.sharding import PartitionSpec as P

NFIB = 64
LAMBDA_COEF = 2.0
SHEAR_CROSS = 1.0
SHEAR_ALONG = 3.0
FIBRE_COEF = 20.0
MASS_COEF = 0.02
FINE_RATIO = 10.0
COARSE_RATIO = 30.0

MESH = pl.DeviceIdType.MESH
HIGHEST = lax.Precision.HIGHEST
LANES = 128
PER = 200
ROWS = 3 * PER
HELD = ROWS + 56
NEIGHBOURS = ((-1, 0), (1, 0), (0, -1), (0, 1), (-1, -1), (-1, 1), (1, -1), (1, 1))
FACE_X, FACE_Y, EDGE = 80, 64, 24
SIZES = (FACE_X, FACE_X, FACE_Y, FACE_Y, EDGE, EDGE, EDGE, EDGE)


def gll_points():
    root = math.sqrt(3.0 / 7.0)
    points = (np.array([-1.0, -root, 0.0, root, 1.0]) + 1.0) / 2.0
    weights = np.array([0.1, 49.0 / 90.0, 32.0 / 45.0, 49.0 / 90.0, 0.1]) / 2.0
    return (points, weights)


def lagrange_slopes(points, where):
    count = len(points)
    table = np.zeros((len(where), count))
    for i, spot in enumerate(where):
        for j in range(count):
            total = 0.0
            for k in range(count):
                if k == j:
                    continue
                term = 1.0 / (points[j] - points[k])
                for m in range(count):
                    if m != j and m != k:
                        term = term * (spot - points[m]) / (points[j] - points[m])
                total = total + term
            table[i, j] = total
    return table


def tables():
    points, weights = gll_points()
    slopes = lagrange_slopes(points, points)
    eye = np.eye(5)
    forward = np.zeros((3, 128, 256))
    weight = np.zeros((128,))
    mass = np.zeros((PER,))
    interp = np.zeros((PER, 8))
    for d in range(3):
        tx, ty, tz = (slopes if d == a else eye for a in range(3))
        full = np.einsum("Jj,Kk,Ii->JKIjki", ty, tz, tx)
        wide = np.zeros((5, 5, 5, 5, 5, 8))
        wide[..., :5] = full
        forward[d, :125, :PER] = wide.reshape(125, PER)
    cube = weights[:, None, None] * weights[None, :, None] * weights[None, None, :]
    weight[:125] = cube.reshape(-1)
    mass_wide = np.zeros((5, 5, 8))
    mass_wide[..., :5] = MASS_COEF * cube
    mass[:] = mass_wide.reshape(-1)
    line = np.stack([1.0 - points, points], 1)
    line8 = np.zeros((8, 2))
    line8[:5] = line
    interp[:] = np.einsum("Jj,Kk,Ii->JKIjki", line, line, line8).reshape(PER, 8)
    gauss = np.array([0.5 - 0.5 / math.sqrt(3.0), 0.5 + 0.5 / math.sqrt(3.0)])
    basis = np.stack([1.0 - gauss, gauss], 1)
    steep = np.array([[-1.0, 1.0], [-1.0, 1.0]])
    coarse = np.zeros((32, 8))
    for d in range(4):
        tx, ty, tz = (steep if d == a else basis for a in range(3))
        coarse[d * 8 : d * 8 + 8] = np.einsum("Jj,Kk,Ii->JKIjki", ty, tz, tx).reshape(8, 8)
    flat = forward.reshape(384, 256)
    parts = (
        flat,
        flat[:, :PER].T,
        np.broadcast_to(weight[:, None], (128, LANES)),
        np.broadcast_to(mass[:, None], (PER, LANES)),
        interp,
        interp.T,
        coarse,
        coarse.T,
    )
    return [jnp.asarray(np.ascontiguousarray(part), dtype=jnp.float32) for part in parts]


def dot(a, b):
    return jnp.dot(a, b, precision=HIGHEST, preferred_element_type=jnp.float32)


def stresses(grad, fibre, scale):
    shear = {}
    for i in range(3):
        for j in range(i, 3):
            shear[i, j] = grad[i][i] if i == j else 0.5 * (grad[i][j] + grad[j][i])
            shear[j, i] = shear[i, j]
    trace = LAMBDA_COEF * (shear[0, 0] + shear[1, 1] + shear[2, 2])
    along = [
        shear[i, 0] * fibre[0] + shear[i, 1] * fibre[1] + shear[i, 2] * fibre[2] for i in range(3)
    ]
    stretch = fibre[0] * along[0] + fibre[1] * along[1] + fibre[2] * along[2]
    half = (0.5 * FIBRE_COEF) * stretch
    cross = 2.0 * (SHEAR_ALONG - SHEAR_CROSS)
    pull = [cross * along[i] + half * fibre[i] for i in range(3)]
    out = {}
    for i in range(3):
        for j in range(i, 3):
            value = 2.0 * SHEAR_CROSS * shear[i, j] + (fibre[i] * pull[j] + pull[i] * fibre[j])
            if i == j:
                value = value + trace
            out[i, j] = out[j, i] = value * scale
    return out


def estimate(n):
    scale = 1.0 / jnp.sqrt(n[0] + 1e-6)
    last = None
    for k in range(1, 4):
        last = jnp.sqrt((n[k] * scale) * scale + 1e-6)
        scale = scale / last
    return last


def smoothing(largest, ratio):
    upper = 1.1 * largest
    lower = upper / ratio
    centre = 0.5 * (upper + lower)
    radius = 0.5 * (upper - lower)
    spread = centre / radius
    weight = 1.0 / spread
    step = [1.0 / centre]
    rest = [jnp.ones_like(largest)]
    total = [jnp.zeros_like(largest)] * 4

    def entry(poly, n):
        return poly[n] if n < len(poly) else jnp.zeros_like(largest)

    for k in range(4):
        total = [total[n] + entry(step, n) for n in range(4)]
        rest = [entry(rest, n) - (step[n - 1] if n > 0 else 0.0) for n in range(k + 2)]
        if k < 3:
            new = 1.0 / (2.0 * spread - weight)
            step = [
                new * weight * entry(step, n) + 2.0 * new / radius * rest[n] for n in range(k + 2)
            ]
            weight = new
    return total, rest


def group_peers(stage, wide, cross):
    chip, row = lax.rem(wide, 8), wide // 8
    if stage == 0:
        return [(row * 8 + lax.rem(chip + k, 8), cross) for k in range(1, 8)]
    spot = row * 4 + cross
    out = []
    for k in range(1, 16):
        other = lax.rem(spot + k, 16)
        out.append((other // 4 * 8 + chip, lax.rem(other, 4)))
    return out


def kernel(
    start_ref, rhs_ref, elem_ref, fwd_ref, bwd_ref, weight_ref, mass_ref, interp_ref, interp_t_ref,
    cgrad_ref, cgrad_t_ref,
    out_ref, cor_ref,
    held, mass_w, grad, send_x, send_y, send_e, got_x, got_y, got_e, csend, cgot, sums, got_a, got_b,
    send_sem, recv_sem, csend_sem, crecv_sem, sum_send, sum_recv,
):
    wide, cross = lax.axis_index("wide"), lax.axis_index("cross")
    n_wide, n_cross = lax.axis_size("wide"), lax.axis_size("cross")

    def present(n):
        dx, dy = NEIGHBOURS[n]
        inside = None
        for here, by, size in ((wide, dx, n_wide), (cross, dy, n_cross)):
            if by:
                ok = here > 0 if by < 0 else here < size - 1
                inside = ok if inside is None else inside & ok
        return inside

    def place(n):
        dx, dy = NEIGHBOURS[n]
        return (wide + dx, cross + dy)

    def opposite(n):
        dx, dy = NEIGHBOURS[n]
        return NEIGHBOURS.index((-dx, -dy))

    got_x[...] = jnp.zeros_like(got_x)
    got_y[...] = jnp.zeros_like(got_y)
    got_e[...] = jnp.zeros_like(got_e)
    cgot[...] = jnp.zeros_like(cgot)
    barrier = pltpu.get_barrier_semaphore()
    expected = jnp.int32(0)
    for n in range(8):
        @pl.when(present(n))
        def _(n=n):
            pl.semaphore_signal(barrier, inc=1, device_id=place(n), device_id_type=MESH)
        expected = expected + present(n).astype(jnp.int32)
    for stage in range(2):
        for peer in group_peers(stage, wide, cross):
            pl.semaphore_signal(barrier, inc=1, device_id=peer, device_id_type=MESH)
            expected = expected + 1

    held[...] = jnp.zeros_like(held)
    send_x[...] = jnp.zeros_like(send_x)
    send_y[...] = jnp.zeros_like(send_y)
    send_e[...] = jnp.zeros_like(send_e)
    sums[...] = jnp.zeros_like(sums)
    mass_w[...] = weight_ref[...] * elem_ref[3:4, :]
    held[0, :ROWS] = start_ref[...]
    pl.semaphore_wait(barrier, expected)

    lane = lax.broadcasted_iota(jnp.int32, (8, LANES), 1)
    sub = lax.broadcasted_iota(jnp.int32, (8, LANES), 0)
    spot = lax.rem(lane, 64)
    low = lane < 64
    one_x = jnp.where(wide < n_wide - 1, 1.0, 0.0)
    one_y = jnp.where(cross < n_cross - 1, 1.0, 0.0)
    keep_y = jnp.where(low, 1.0, one_y)

    def spread_to(mask, rows):
        return jnp.broadcast_to(mask[:1], (rows, LANES))

    def sides(s, n):
        if n < 2:
            return send_x.at[s, n], got_x.at[s, n], got_x.at[s, opposite(n)]
        if n < 4:
            return send_y.at[s, n - 2], got_y.at[s, n - 2], got_y.at[s, opposite(n) - 2]
        return send_e.at[s, n - 4], got_e.at[s, n - 4], got_e.at[s, opposite(n) - 4]

    def outgoing(s, n):
        source, _, target = sides(s, n)
        return pltpu.make_async_remote_copy(
            src_ref=source, dst_ref=target, send_sem=send_sem.at[s, n],
            recv_sem=recv_sem.at[s, opposite(n)], device_id=place(n), device_id_type=MESH)

    def incoming(s, n):
        source, target, _ = sides(s, n)
        return pltpu.make_async_remote_copy(
            src_ref=source, dst_ref=target, send_sem=send_sem.at[s, n],
            recv_sem=recv_sem.at[s, n], device_id=place(n), device_id_type=MESH)

    def exchange(t, s):
        for side in range(2):
            send_x[s, side, :75] = held[t, pl.ds(4 * side, 75, stride=8)]
            face = jnp.concatenate(
                [held[t, c * PER + side * 160 : c * PER + side * 160 + 40] for c in range(3)], 0)
            first, second = face[:64], face[64:]
            rolled = pltpu.roll(second, 64, 1)
            use = spread_to(low if side == 0 else ~low, 56)
            send_y[s, side, :56] = jnp.where(use, first[:56], rolled)
            send_y[s, side, 56:] = first[56:]
        for n in range(4, 8):
            dx, dy = NEIGHBOURS[n]
            i, j = (4 if dx > 0 else 0), (4 if dy > 0 else 0)
            for c in range(3):
                send_e[s, n - 4, c * 8 : c * 8 + 5] = held[
                    t, pl.ds(c * PER + j * 40 + i, 5, stride=8)]
        for n in (4, 5, 6, 7, 0, 1, 2, 3):
            @pl.when(present(n))
            def _(n=n):
                outgoing(s, n).start()
        for n in range(8):
            @pl.when(present(n))
            def _(n=n):
                incoming(s, n).wait_recv()
        for side in range(2):
            got = got_y[s, side]
            use = spread_to(low if side == 0 else ~low, 64)
            first = jnp.where(use, pltpu.roll(got, 64, 1), 0.0)
            second = jnp.where(use[:56], got[:56], 0.0)
            more = jnp.concatenate([first, second], 0)
            for c in range(3):
                at = c * PER + side * 160
                value = held[t, at : at + 40] + more[c * 40 : c * 40 + 40]
                held[t, at : at + 40] = value
        for side in range(2):
            value = held[t, pl.ds(4 * side, 75, stride=8)] + got_x[s, side, :75]
            held[t, pl.ds(4 * side, 75, stride=8)] = value
        for n in range(4, 8):
            dx, dy = NEIGHBOURS[n]
            i, j = (4 if dx > 0 else 0), (4 if dy > 0 else 0)
            use = low if dy < 0 else ~low
            for c in range(3):
                more = jnp.where(use, pltpu.roll(got_e[s, n - 4, c * 8 : c * 8 + 8], 64, 1), 0.0)
                at = pl.ds(c * PER + j * 40 + i, 5, stride=8)
                held[t, at] = held[t, at] + more[:5]
        held[t, pl.ds(4, 75, stride=8)] = held[t, pl.ds(4, 75, stride=8)] * one_x
        for c in range(3):
            at = c * PER + 160
            held[t, at : at + 40] = held[t, at : at + 40] * spread_to(keep_y, 40)
        for n in range(8):
            @pl.when(present(n))
            def _(n=n):
                outgoing(s, n).wait_send()

    fibre = [elem_ref[i : i + 1, :] for i in range(3)]

    def elements(t):
        block = jnp.concatenate([held[t, c * PER : c * PER + 256] for c in range(3)], 1)
        grad[...] = dot(fwd_ref[...], block)

        def tile(q, carry):
            at = pl.multiple_of(q * 16, 16)
            g = [[grad[pl.ds(d * 128 + at, 16), c * 128 : c * 128 + 128] for d in range(3)]
                 for c in range(3)]
            part = stresses(g, fibre, mass_w[pl.ds(at, 16), :])
            for c in range(3):
                for d in range(3):
                    grad[pl.ds(d * 128 + at, 16), c * 128 : c * 128 + 128] = part[c, d]
            return carry

        lax.fori_loop(0, 8, tile, 0, unroll=True)
        result = dot(bwd_ref[...], grad[...])
        return [
            result[:, c * 128 : c * 128 + 128] + mass_ref[...] * held[t, c * PER : c * PER + PER]
            for c in range(3)
        ]

    inner = spread_to(spot > 0, 8)
    outer = spread_to(spot < 63, 8)

    def gather_local(t):
        for c in range(3):
            for j in range(5):
                at = c * PER + j * 40
                first, last = held[t, at : at + 8], held[t, at + 32 : at + 40]
                held[t, at : at + 8] = first + jnp.where(inner, pltpu.roll(last, 1, 1), 0.0)
                held[t, at + 32 : at + 40] = last + jnp.where(outer, pltpu.roll(first, 127, 1), 0.0)
            at = c * PER
            first, last = held[t, at : at + 40], held[t, at + 160 : at + 200]
            use = spread_to(low, 40)
            held[t, at : at + 40] = first + jnp.where(use, 0.0, pltpu.roll(last, 64, 1))
            held[t, at + 160 : at + 200] = last + jnp.where(use, pltpu.roll(first, 64, 1), 0.0)

    ends = spread_to(spot == 63, 8)

    def square(t):
        total = jnp.zeros((8, LANES), jnp.float32)
        tail = jnp.zeros((8, LANES), jnp.float32)
        for c in range(3):
            for j in range(4):
                for k in range(5):
                    at = c * PER + j * 40 + k * 8
                    v = held[t, at : at + 8]
                    if k < 4:
                        total = total + v * v
                    else:
                        tail = tail + v * v
        total = total + jnp.where(ends, tail, 0.0)
        total = jnp.where(sub < 4, total, 0.0)
        return jnp.sum(total, axis=0, keepdims=True)

    def all_sum(slot):
        for stage in range(2):
            got = (got_a, got_b)[stage]
            copies = [
                pltpu.make_async_remote_copy(
                    src_ref=sums.at[slot, stage], dst_ref=got.at[slot, k],
                    send_sem=sum_send.at[slot, stage, k], recv_sem=sum_recv.at[slot, stage, k],
                    device_id=peer, device_id_type=MESH)
                for k, peer in enumerate(group_peers(stage, wide, cross))
            ]
            for copy in copies:
                copy.start()
            for copy in copies:
                copy.wait_recv()
            total = sums[slot, stage]
            for k in range(len(copies)):
                total = total + got[slot, k]
            for copy in copies:
                copy.wait_send()
            if stage == 0:
                sums[slot, 1] = total
        return jnp.sum(total, axis=1, keepdims=True)

    def four_steps(base):
        def step(t, carry):
            parts = elements(t)
            for c in range(3):
                at = c * PER
                held[t + 1, at : at + PER] = parts[c]
            gather_local(t + 1)

            @pl.when(t == 0)
            def _():
                held[1, :ROWS] = rhs_ref[...] - held[1, :ROWS]

            exchange(t + 1, lax.rem(t + base, 2))
            return carry

        lax.fori_loop(0, 4, step, 0)

    exchange(0, 0)
    four_steps(1)
    for n in range(4):
        sums[0, 0, n : n + 1] = square(n + 1)
    norms = all_sum(0)
    largest = jnp.broadcast_to(estimate([norms[n : n + 1] for n in range(4)]), (1, LANES))
    step_poly, rest_poly = smoothing(largest, FINE_RATIO)

    parts = elements(4)
    row = lax.broadcasted_iota(jnp.int32, (PER, LANES), 0)
    wide_lane = lax.broadcasted_iota(jnp.int32, (PER, LANES), 1)
    at_i, at_k, at_j = lax.rem(row, 8), lax.rem(row // 8, 5), row // 40
    owned = (at_i < 4) & (at_j < 4) & ((at_k < 4) | (lax.rem(wide_lane, 64) == 63))
    free = ((at_i < 4) | (wide < n_wide - 1)) & (
        (at_j < 4) | (wide_lane < 64) | (cross < n_cross - 1))
    for c in range(3):
        at = c * PER
        kept = [held[n + 1, at : at + PER] for n in range(4)]
        value = rest_poly[0] * kept[0]
        more = step_poly[0] * kept[0]
        for n in range(1, 4):
            value = value + rest_poly[n] * kept[n]
            more = more + step_poly[n] * kept[n]
        value = jnp.where(owned, value, 0.0) + jnp.where(free, rest_poly[4] * parts[c], 0.0)
        held[0, at : at + PER] = held[0, at : at + PER] + more
        csend[0, c * 8 : c * 8 + 8] = dot(interp_t_ref[...], value)

    bit_i, bit_k, bit_j = lax.rem(sub, 2) == 1, lax.rem(sub // 2, 2) == 1, sub >= 4
    drop = (bit_i & (wide == n_wide - 1)) | (bit_j & ~low & (cross == n_cross - 1))
    cfree = jnp.where(drop, 0.0, 1.0)

    def swap(v, by, bit):
        return jnp.where(bit, pltpu.roll(v, by, 0), pltpu.roll(v, 8 - by, 0))

    def coarse_copy(s, n, m):
        return pltpu.make_async_remote_copy(
            src_ref=csend.at[s], dst_ref=cgot.at[s, m], send_sem=csend_sem.at[s, n],
            recv_sem=crecv_sem.at[s, m], device_id=place(n), device_id_type=MESH)

    def coarse_exchange(s):
        for c in range(3):
            v = csend[s, c * 8 : c * 8 + 8]
            other = swap(v, 2, bit_k)
            v = v + jnp.where(
                bit_k, jnp.where(spot < 63, pltpu.roll(other, 127, 1), 0.0),
                jnp.where(spot > 0, pltpu.roll(other, 1, 1), 0.0))
            other = pltpu.roll(swap(v, 4, bit_j), 64, 1)
            v = v + jnp.where(bit_j == low, other, 0.0)
            csend[s, c * 8 : c * 8 + 8] = v
        for n in (4, 5, 6, 7, 0, 1, 2, 3):
            @pl.when(present(n))
            def _(n=n):
                coarse_copy(s, n, opposite(n)).start()
        for n in range(8):
            @pl.when(present(n))
            def _(n=n):
                coarse_copy(s, n, n).wait_recv()
        out = []
        for c in range(3):
            v = csend[s, c * 8 : c * 8 + 8]
            for n in range(8):
                dx, dy = NEIGHBOURS[n]
                got = cgot[s, n, c * 8 : c * 8 + 8]
                use = None
                if dx:
                    got = swap(got, 1, bit_i)
                    use = bit_i if dx > 0 else ~bit_i
                if dy:
                    got = pltpu.roll(swap(got, 4, bit_j), 64, 1)
                    side = (bit_j & ~low) if dy > 0 else (~bit_j & low)
                    use = side if use is None else use & side
                v = v + jnp.where(use, got, 0.0)
            out.append(v * cfree)
        for n in range(8):
            @pl.when(present(n))
            def _(n=n):
                coarse_copy(s, n, opposite(n)).wait_send()
        return out

    coarse_scale = 0.125 * elem_ref[3:4, :]

    def coarse_elements(vec, s):
        block = jnp.concatenate(vec, 1)
        g = dot(cgrad_ref[...], block)
        part = stresses(
            [[g[d * 8 : d * 8 + 8, c * 128 : c * 128 + 128] for d in range(3)] for c in range(3)],
            fibre, coarse_scale)
        for c in range(3):
            stack = jnp.concatenate(
                [part[c, d] for d in range(3)]
                + [(0.125 * MASS_COEF) * g[24:32, c * 128 : c * 128 + 128]], 0)
            csend[s, c * 8 : c * 8 + 8] = dot(cgrad_t_ref[...], stack)

    own_c = ~bit_i & ~bit_j & (~bit_k | (spot == 63))

    def coarse_square(vec):
        total = vec[0] * vec[0] + vec[1] * vec[1] + vec[2] * vec[2]
        return jnp.sum(jnp.where(own_c, total, 0.0), axis=0, keepdims=True)

    vectors = [coarse_exchange(0)]
    sums[1, 0, 0:1] = coarse_square(vectors[0])
    for n in range(1, 4):
        coarse_elements(vectors[-1], n % 2)
        vectors.append(coarse_exchange(n % 2))
        sums[1, 0, n : n + 1] = coarse_square(vectors[-1])
    norms = all_sum(1)
    coarse_largest = jnp.broadcast_to(estimate([norms[n : n + 1] for n in range(4)]), (1, LANES))
    coarse_poly, _ = smoothing(coarse_largest, COARSE_RATIO)
    for c in range(3):
        value = coarse_poly[0] * vectors[0][c]
        for n in range(1, 4):
            value = value + coarse_poly[n] * vectors[n][c]
        cor_ref[c * 8 : c * 8 + 8] = value
        at = c * PER
        held[0, at : at + PER] = held[0, at : at + PER] + dot(interp_ref[...], value)

    four_steps(1)
    for c in range(3):
        at = c * PER
        value = held[0, at : at + PER]
        for n in range(4):
            value = value + step_poly[n] * held[n + 1, at : at + PER]
        out_ref[at : at + PER] = value


def to_rows(field):
    z = jnp.concatenate(
        [field[..., :-1].reshape(3, 4, 8, 64, 4), field[..., 4::4][..., None]], -1)
    z = jnp.pad(z, ((0, 0), (0, 4), (0, 1), (0, 0), (0, 0)))
    y = jnp.stack([z[:, :, :5], z[:, :, 4:]], 2)
    return jnp.transpose(y, (0, 3, 5, 1, 2, 4)).reshape(ROWS, LANES)


def from_rows(rows):
    view = rows.reshape(3, 5, 5, 8, 2, 64)[:, :4, :, :4]
    view = jnp.transpose(view, (0, 3, 4, 1, 5, 2)).reshape(3, 4, 8, 64, 5)
    return jnp.concatenate(
        [view[..., :4].reshape(3, 4, 8, 256), view[:, :, :, -1:, 4]], -1)


def fibre_vectors(index):
    angle = index.astype(jnp.float32) * (2.0 * math.pi / NFIB)
    tilt = 0.4 * jnp.sin(3.0 * angle)
    return jnp.stack(
        [jnp.cos(angle) * jnp.cos(tilt), jnp.sin(angle) * jnp.cos(tilt), jnp.sin(tilt)]
    )


def on_device(rhs, start, stiffness, fibre_index):
    fibre = fibre_vectors(fibre_index).reshape(3, LANES)
    elem = jnp.concatenate([fibre, stiffness.reshape(1, LANES), jnp.zeros((4, LANES))], 0)
    operands = [to_rows(start), to_rows(rhs), elem] + tables()
    vmem = pl.BlockSpec(memory_space=pltpu.VMEM)
    f32 = jnp.float32
    rows, coarse = pl.pallas_call(
        kernel,
        out_shape=(
            jax.ShapeDtypeStruct((ROWS, LANES), f32),
            jax.ShapeDtypeStruct((24, LANES), f32),
        ),
        in_specs=[vmem] * len(operands),
        out_specs=(vmem, vmem),
        scratch_shapes=[
            pltpu.VMEM((5, HELD, LANES), f32),
            pltpu.VMEM((128, LANES), f32),
            pltpu.VMEM((384, 384), f32),
            pltpu.VMEM((2, 2, FACE_X, LANES), f32),
            pltpu.VMEM((2, 2, FACE_Y, LANES), f32),
            pltpu.VMEM((2, 4, EDGE, LANES), f32),
            pltpu.VMEM((2, 2, FACE_X, LANES), f32),
            pltpu.VMEM((2, 2, FACE_Y, LANES), f32),
            pltpu.VMEM((2, 4, EDGE, LANES), f32),
            pltpu.VMEM((2, 24, LANES), f32),
            pltpu.VMEM((2, 8, 24, LANES), f32),
            pltpu.VMEM((2, 2, 8, LANES), f32),
            pltpu.VMEM((2, 7, 8, LANES), f32),
            pltpu.VMEM((2, 15, 8, LANES), f32),
            pltpu.SemaphoreType.DMA((2, 8)),
            pltpu.SemaphoreType.DMA((2, 8)),
            pltpu.SemaphoreType.DMA((2, 8)),
            pltpu.SemaphoreType.DMA((2, 8)),
            pltpu.SemaphoreType.DMA((2, 2, 15)),
            pltpu.SemaphoreType.DMA((2, 2, 15)),
        ],
        compiler_params=pltpu.CompilerParams(
            collective_id=0, has_side_effects=True, vmem_limit_bytes=32 * 1024 * 1024
        ),
    )(*operands)
    view = coarse.reshape(3, 2, 2, 2, 2, 64)[:, 0, :, 0]
    correction = jnp.concatenate([view[:, 0], view[:, 1, :, -1:]], -1)[:, None]
    return from_rows(rows), correction


def solution(mesh):
    in_specs = (
        P(None, "wide", "cross", None),
        P(None, "wide", "cross", None),
        P("wide", "cross", None),
        P("wide", "cross", None),
    )
    out_specs = (P(None, "wide", "cross", None), P(None, "wide", "cross", None))
    return jax.shard_map(
        on_device, mesh=mesh, in_specs=in_specs, out_specs=out_specs, check_vma=False
    )
```

time: 1690 us -> 110 us (0.07); the launches traced: 1650 us -> 110 us
  blocking collectives: 524 us -> 0 us
  local copies, waits for them, and re-layouts: 512 us -> 10.7 us
  starting transfers between devices: 204 us -> 0 us
  waiting for transfers between devices: 188 us -> 0 us
  matrix products: 131 us -> 0 us
  Pallas kernels: 0 us -> 96.1 us
  other arithmetic: 80.7 us -> 1.72 us
    psum x8 -> x0, blocking collectives: 524 us -> none  [the longest x4 264 us: fine_total(): return lax.psum(jnp.sum(field * field), ('wide', 'cross'))]
    slice x211 -> x12, local copies, waits for them, and re-layouts: 404 us -> 6.08 us  [the longest x2 3.34 us: to_rows(): field[..., 4::4][..., None]]
    ppermute x76 -> x0, starting transfers between devices: 204 us -> none  [passed_along(): return lax.ppermute(block, axis, route)]
    ppermute x76 -> x0, waiting for transfers between devices: 188 us -> none  [passed_along(): return lax.ppermute(block, axis, route)]
    dot_general x600 -> x0, matrix products: 131 us -> none  [the longest x594 129 us: contract(): jnp.einsum(forms[axis], table, field, precision=lax.Precision.HIGHEST)]
    pallas_call x0 -> x1, Pallas kernels: none -> 96.1 us  [on_device(): pl.pallas_call(kernel, out_shape=(jax.ShapeDtypeStruct((ROWS, LANES), f32...]
    transpose x108 -> x2, other arithmetic: 45.7 us -> 0.09 us  [to_rows(): return jnp.transpose(y, (0, 3, 5, 1, 2, 4)).reshape(ROWS, LANES)]
    broadcast_in_dim x33 -> x1, local copies, waits for them, and re-layouts: 38.9 us -> 0.01 us  [on_device(): jnp.zeros((4, LANES))]
  transfers between devices with their start and end apart: 76 -> 0, of which waited for: 76 -> 0; matrix products, arithmetic and copies ran while one was open for 0% -> 0% of each run, Pallas kernels for 0% -> 0%
where the time goes in v1:
time: 110 us
  Pallas kernels  96.1 us (87%)
  local copies, waits for them, and re-layouts  10.7 us (10%)
  other arithmetic  1.72 us (2%)
    pallas_call x1, Pallas kernels, on_device(): pl.pallas_call(kernel, out_shape=(jax.ShapeDtypeStruct((ROWS, LANES), f32...  96.1 us
    slice x2, local copies, waits for them, and re-layouts, to_rows(): field[..., 4::4][..., None]  3.34 us

profile of v1, /device:TPU:7, one launch (start us, length us, event | category | flops | bytes accessed | tf_op | source)
XLA Modules:
  0.0 109.5 jit_solution(6250494031731503147)
XLA Ops:
  0.6 2.3 %slice.43 = f32[3,4,8,64]{3,2,1,0:T(8,128)S(1)} slice(f32[3,4,8,257]{3,2,1,0:T(8,128)} %param.13), slice={[0:3:1], [0:4:1], [0:8:1], [4:257:4]} | slice | bytes 49152 | tf_op jit(solution)/shard_map/slice | solution.py:536
  2.9 0.9 slice.42
  3.8 0.5 copy.52
  4.3 0.6 copy.53
  4.9 0.1 select_maximum_fusion.1
  5.0 0.1 slice_bitcast_fusion.3
  5.1 0.1 copy.55
  5.2 0.1 copy.54
  5.2 0.0 copy-start.8
  5.2 0.0 slice-start
  5.3 0.3 copy.56
  5.6 0.3 reshape.39.start_ref
  6.0 0.2 copy-done.8
  6.1 1.1 slice.47
  7.2 0.0 slice-done
  7.2 0.5 copy.57
  7.7 0.6 copy.58
  8.3 0.1 select_maximum_fusion
  8.4 0.1 slice_bitcast_fusion.1
  8.5 0.1 copy.60
  8.5 0.1 copy.59
  8.6 0.0 copy-start.9
  8.6 0.0 copy-start.10
  8.6 0.0 copy-start
  8.6 0.0 copy-start.1
  8.6 0.0 copy-start.2
  8.7 0.0 copy-start.3
  8.7 0.0 copy-start.4
  8.7 0.0 copy-start.5
  8.7 0.0 copy-start.6
  8.7 0.0 copy-start.7
  8.8 0.3 copy.61
  9.1 0.3 reshape.41.rhs_ref
  9.4 0.0 copy-done.9
  9.5 0.1 fusion
  9.5 0.1 stack.34
  9.6 0.1 stack.35
  9.7 0.1 stack.36
  9.8 0.0 copy-done.10
  9.8 0.1 reshape.42
  9.9 0.0 copy-done
  9.9 0.0 copy-done.1
  9.9 0.0 copy-done.2
  9.9 0.0 copy-done.3
  9.9 0.0 copy-done.4
  10.0 0.0 copy-done.5
  10.0 0.0 copy-done.6
  10.0 0.0 copy-done.7
  10.0 96.1 %shard_map.131 = (f32[600,128]{1,0:T(8,128)S(1)}, f32[24,128]{1,0:T(8,128)S(1)}) custom-call(f32[600,128]{1,0:T(8,128)S(1)} %reshape.39.start_ref, f32[600,128]{1,0:T(8,128)S(1)} %reshape.41.rhs_ref, f32[8,128]{1,0:T(8,128)S(1)} %concatenate.19.elem_ref, f32[384,256]{1,0:T(8,128)S(1)} %copy-done, f32[200,384]{1,0:T(8,128)S(1)} %copy-done.1, ...), custom_call_target="tpu_custom_call" | custom-call | tf_op jit(solution)/shard_map/pallas_call | solution.py:563
  106.1 0.4 reshape.43
  106.5 0.1 copy.69
  106.6 0.1 slice_bitcast_fusion.4
  106.7 0.7 copy.63
  107.4 0.4 copy.64
  107.8 0.7 pad_maximum_fusion
  108.5 0.1 reshape.46
  108.6 0.1 slice.65
  108.7 0.1 copy.67
  108.8 0.1 copy.68
  108.9 0.7 maximum_bitcast_fusion.2
  (8 shorter events, 0.2 us)
Async XLA Ops:
  5.2 0.9 copy-start.8
  5.2 2.0 %slice-start = ((f32[3,4,8,257]{3,2,1,0:T(8,128)}), f32[3,4,8,256]{3,2,1,0:T(8,128)S(1)}, s32[]{:S(2)}) async-start(f32[3,4,8,257]{3,2,1,0:T(8,128)} %param.12), calls=%async_computation | async-start | bytes 196608 | tf_op jit(solution)/shard_map/slice | solution.py:536
  8.6 0.9 copy-start.9
  8.6 1.2 %copy-start.10 = (f32[1,2,64]{2,1,0:T(2,128)S(1)}, f32[1,2,64]{2,1,0:T(2,128)}, u32[]{:S(2)}) copy-start(f32[1,2,64]{2,1,0:T(2,128)} %param.14) | copy-start | bytes 1540
  8.6 1.3 %copy-start = (f32[384,256]{1,0:T(8,128)S(1)}, f32[384,256]{1,0:T(8,128)}, u32[]{:S(2)}) copy-start(f32[384,256]{1,0:T(8,128)} %constant.27.clone.fwd_ref) | copy-start | bytes 1179652
  8.6 1.3 %copy-start.1 = (f32[200,384]{1,0:T(8,128)S(1)}, f32[200,384]{1,0:T(8,128)}, u32[]{:S(2)}) copy-start(f32[200,384]{1,0:T(8,128)} %constant.28.clone.bwd_ref) | copy-start | bytes 921604
  8.6 1.3 %copy-start.2 = (f32[200,128]{1,0:T(8,128)S(1)}, f32[200,128]{1,0:T(8,128)}, u32[]{:S(2)}) copy-start(f32[200,128]{1,0:T(8,128)} %constant.30.clone.mass_ref) | copy-start | bytes 307204
  8.7 1.3 %copy-start.3 = (f32[200,8]{1,0:T(8,128)S(1)}, f32[200,8]{1,0:T(8,128)}, u32[]{:S(2)}) copy-start(f32[200,8]{1,0:T(8,128)} %constant.31.clone.interp_ref) | copy-start | bytes 19204
  8.7 1.3 %copy-start.4 = (f32[128,128]{1,0:T(8,128)S(1)}, f32[128,128]{1,0:T(8,128)}, u32[]{:S(2)}) copy-start(f32[128,128]{1,0:T(8,128)} %constant.29.clone.weight_ref) | copy-start | bytes 196612
  8.7 1.3 %copy-start.5 = (f32[32,8]{1,0:T(8,128)S(1)}, f32[32,8]{1,0:T(8,128)}, u32[]{:S(2)}) copy-start(f32[32,8]{1,0:T(8,128)} %constant.33.clone.cgrad_ref) | copy-start | bytes 3076
  8.7 1.3 %copy-start.6 = (f32[8,200]{1,0:T(8,128)S(1)}, f32[8,200]{1,0:T(8,128)}, u32[]{:S(2)}) copy-start(f32[8,200]{1,0:T(8,128)} %constant.32.clone.interp_t_ref) | copy-start | bytes 19204
  8.7 1.3 %copy-start.7 = (f32[8,32]{1,0:T(8,128)S(1)}, f32[8,32]{1,0:T(8,128)}, u32[]{:S(2)}) copy-start(f32[8,32]{1,0:T(8,128)} %constant.34.clone.cgrad_t_ref) | copy-start | bytes 3076

commit v2 on v1

v2 whole, which is shorter than its diff:
```python
import functools
import math

import jax
import jax.numpy as jnp
import numpy as np
from jax import lax
from jax.experimental import pallas as pl
from jax.experimental.pallas import tpu as pltpu
from jax.sharding import PartitionSpec as P

NFIB = 64
LAMBDA_COEF = 2.0
SHEAR_CROSS = 1.0
SHEAR_ALONG = 3.0
FIBRE_COEF = 20.0
MASS_COEF = 0.02
FINE_RATIO = 10.0
COARSE_RATIO = 30.0

MESH = pl.DeviceIdType.MESH
LANES = 128
PER = 200
ROWS = 3 * PER
NEIGHBOURS = ((-1, 0), (1, 0), (0, -1), (0, 1), (-1, -1), (-1, 1), (1, -1), (1, 1))
FACE_X, FACE_Y, EDGE = 80, 64, 24
REACH = (-4, -3, -2, -1, 1, 2, 3, 4)
HOME = 3


def gll_points():
    root = math.sqrt(3.0 / 7.0)
    points = (np.array([-1.0, -root, 0.0, root, 1.0]) + 1.0) / 2.0
    weights = np.array([0.1, 49.0 / 90.0, 32.0 / 45.0, 49.0 / 90.0, 0.1]) / 2.0
    return (points, weights)


def lagrange_slopes(points, where):
    count = len(points)
    table = np.zeros((len(where), count))
    for i, spot in enumerate(where):
        for j in range(count):
            total = 0.0
            for k in range(count):
                if k == j:
                    continue
                term = 1.0 / (points[j] - points[k])
                for m in range(count):
                    if m != j and m != k:
                        term = term * (spot - points[m]) / (points[j] - points[m])
                total = total + term
            table[i, j] = total
    return table


def tables():
    points, weights = gll_points()
    slopes = lagrange_slopes(points, points)
    cube = np.zeros((5, 5, 8))
    cube[..., :5] = weights[:, None, None] * weights[None, :, None] * weights[None, None, :]
    columns = np.zeros((12, 8, LANES))
    columns[0:5, :5] = slopes.T[:, :, None]
    columns[5:10, :5] = slopes[:, :, None]
    columns[10, :5] = (1.0 - points)[:, None]
    columns[11, :5] = points[:, None]
    parts = (
        np.broadcast_to(cube.reshape(-1)[:, None], (PER, LANES)),
        columns.reshape(96, LANES),
    )
    return [jnp.asarray(np.ascontiguousarray(part), dtype=jnp.float32) for part in parts]


def dot(a, b):
    return jnp.dot(
        a, b, precision=lax.Precision.HIGHEST, preferred_element_type=jnp.float32
    )


GAUSS = 0.5 / math.sqrt(3.0)


def to_gauss(u0, u1):
    slope = u1 - u0
    middle = u0 + 0.5 * slope
    part = GAUSS * slope
    return middle - part, middle + part, slope


def from_gauss(a0, a1, slope=None):
    both = a0 + a1
    last = 0.5 * both + GAUSS * (a1 - a0)
    if slope is not None:
        last = last + slope
    return both - last, last


def along_line(u, table):
    half = lambda i, j: 0.5 * (float(table[i, j]) + float(table[i, 4 - j]))
    odd_half = lambda i, j: 0.5 * (float(table[i, j]) - float(table[i, 4 - j]))
    even = [u[0] + u[4], u[1] + u[3]]
    odd = [u[0] - u[4], u[1] - u[3]]
    p = [
        half(i, 0) * even[0] + half(i, 1) * even[1] + float(table[i, 2]) * u[2] for i in range(2)
    ]
    q = [odd_half(i, 0) * odd[0] + odd_half(i, 1) * odd[1] for i in range(3)]
    return [q[0] + p[0], q[1] + p[1], q[2], q[1] - p[1], q[0] - p[0]]


def stresses(grad, fibre, scale):
    shear = {}
    for i in range(3):
        for j in range(i, 3):
            shear[i, j] = grad[i][i] if i == j else 0.5 * (grad[i][j] + grad[j][i])
            shear[j, i] = shear[i, j]
    trace = LAMBDA_COEF * (shear[0, 0] + shear[1, 1] + shear[2, 2])
    along = [
        shear[i, 0] * fibre[0] + shear[i, 1] * fibre[1] + shear[i, 2] * fibre[2] for i in range(3)
    ]
    stretch = fibre[0] * along[0] + fibre[1] * along[1] + fibre[2] * along[2]
    half = (0.5 * FIBRE_COEF) * stretch
    cross = 2.0 * (SHEAR_ALONG - SHEAR_CROSS)
    pull = [cross * along[i] + half * fibre[i] for i in range(3)]
    out = {}
    for i in range(3):
        for j in range(i, 3):
            value = 2.0 * SHEAR_CROSS * shear[i, j] + (fibre[i] * pull[j] + pull[i] * fibre[j])
            if i == j:
                value = value + trace
            out[i, j] = out[j, i] = value * scale
    return out


def estimate(n):
    scale = 1.0 / jnp.sqrt(n[0] + 1e-6)
    last = None
    for k in range(1, 4):
        last = jnp.sqrt((n[k] * scale) * scale + 1e-6)
        scale = scale / last
    return last


def smoothing(largest, ratio):
    upper = 1.1 * largest
    lower = upper / ratio
    centre = 0.5 * (upper + lower)
    radius = 0.5 * (upper - lower)
    spread = centre / radius
    weight = 1.0 / spread
    step = [1.0 / centre]
    rest = [jnp.ones_like(largest)]
    total = [jnp.zeros_like(largest)] * 4

    def entry(poly, n):
        return poly[n] if n < len(poly) else jnp.zeros_like(largest)

    for k in range(4):
        total = [total[n] + entry(step, n) for n in range(4)]
        rest = [entry(rest, n) - (step[n - 1] if n > 0 else 0.0) for n in range(k + 2)]
        if k < 3:
            new = 1.0 / (2.0 * spread - weight)
            step = [
                new * weight * entry(step, n) + 2.0 * new / radius * rest[n] for n in range(k + 2)
            ]
            weight = new
    return total, rest


def kernel(
    start_ref, rhs_ref, elem_ref, weight_ref, column_ref,
    out_ref, cor_ref,
    held, load, mass_w, slope_y, flux_x, flux_y, planes,
    send_x, send_y, send_e, got_x, got_y, got_e,
    rest, coarse_out, reach_in, elem_z, elem_out, elem_in, elem_c, vertex, gather,
    sums, got_z, got_w,
    send_sem, recv_sem, z_send, z_recv, w_send, w_recv, ez_send, ez_recv, cz_send, cz_recv,
    er_send, er_recv, cr_send, cr_recv,
):
    wide, cross = lax.axis_index("wide"), lax.axis_index("cross")
    n_wide, n_cross = lax.axis_size("wide"), lax.axis_size("cross")
    f32 = jnp.float32

    def within(at, by, size):
        return at >= -by if by < 0 else at < size - by

    def present(n):
        dx, dy = NEIGHBOURS[n]
        inside = None
        for here, by, size in ((wide, dx, n_wide), (cross, dy, n_cross)):
            if by:
                ok = within(here, by, size)
                inside = ok if inside is None else inside & ok
        return inside

    def place(n):
        dx, dy = NEIGHBOURS[n]
        return (wide + dx, cross + dy)

    def opposite(n):
        dx, dy = NEIGHBOURS[n]
        return NEIGHBOURS.index((-dx, -dy))

    z_peers = [(wide, lax.rem(cross + k, n_cross)) for k in range(1, n_cross)]
    w_peers = [(lax.rem(wide + k, n_wide), cross) for k in range(1, n_wide)]

    got_x[...] = jnp.zeros_like(got_x)
    got_y[...] = jnp.zeros_like(got_y)
    got_e[...] = jnp.zeros_like(got_e)
    reach_in[...] = jnp.zeros_like(reach_in)
    elem_in[...] = jnp.zeros_like(elem_in)
    barrier = pltpu.get_barrier_semaphore()
    expected = jnp.int32(len(z_peers) + len(w_peers))
    for peer in z_peers + w_peers:
        pl.semaphore_signal(barrier, inc=1, device_id=peer, device_id_type=MESH)
    for n in range(4, 8):
        @pl.when(present(n))
        def _(n=n):
            pl.semaphore_signal(barrier, inc=1, device_id=place(n), device_id_type=MESH)
        expected = expected + present(n).astype(jnp.int32)

    lane = lax.broadcasted_iota(jnp.int32, (8, LANES), 1)
    sub = lax.broadcasted_iota(jnp.int32, (8, LANES), 0)
    spot = lax.rem(lane, 64)
    low = lane < 64
    ends = spot == 63
    one_x = jnp.where(wide < n_wide - 1, 1.0, 0.0)
    one_y = jnp.where(cross < n_cross - 1, 1.0, 0.0)
    keep_y = jnp.where(low, 1.0, one_y)

    def spread_to(mask, rows):
        return jnp.broadcast_to(mask[:1], (rows, LANES))

    send_x[...] = jnp.zeros_like(send_x)
    send_e[...] = jnp.zeros_like(send_e)
    sums[...] = jnp.zeros_like(sums)
    vertex[...] = jnp.zeros_like(vertex)
    gather[...] = jnp.zeros_like(gather)
    mass_w[...] = weight_ref[...] * elem_ref[3:4, :]
    elem_z[cross] = elem_ref[...]

    z_at = lax.broadcasted_iota(jnp.int32, (256, 5 * LANES), 0)
    col = lax.broadcasted_iota(jnp.int32, (256, 5 * LANES), 1)
    pick = jnp.where(z_at == 4 * lax.rem(col, 64) + col // LANES, 1.0, 0.0)

    def unpack(ref, into):
        nodes = dot(ref[:, :, :, 0:256].reshape(96, 256), pick)
        final = jnp.broadcast_to(ref[:, :, :, 256:257].reshape(96, 1), (96, LANES))
        for k in range(5):
            part = nodes[:, k * LANES : k * LANES + LANES]
            planes[k] = jnp.where(spread_to(ends, 96), final, part) if k == 4 else part
        into[...] = jnp.zeros_like(into)
        for c in range(3):
            for j in range(5):
                for k in range(5):
                    first = planes[k, pl.ds(c * 32 + j, 4, stride=8)]
                    if j < 4:
                        second = planes[k, pl.ds(c * 32 + 4 + j, 4, stride=8)]
                    else:
                        second = jnp.zeros((4, LANES), f32)
                    at = c * PER + j * 40 + k * 8
                    into[at : at + 4] = jnp.where(low[:4], first, second)

    unpack(start_ref, held.at[0])
    pl.semaphore_wait(barrier, expected)

    def z_copy(source, target, sem_out, sem_in, k, back=False):
        return pltpu.make_async_remote_copy(
            src_ref=source, dst_ref=target, send_sem=sem_out.at[k - 1], recv_sem=sem_in.at[k - 1],
            device_id=z_peers[k - 1], device_id_type=MESH)

    def from_z(k):
        return lax.rem(cross + n_cross - k, n_cross)

    def reach_out(source, into, sem_out, sem_in, m):
        back = REACH.index(-REACH[m])
        return pltpu.make_async_remote_copy(
            src_ref=source, dst_ref=into.at[back], send_sem=sem_out.at[m], recv_sem=sem_in.at[back],
            device_id=(wide + REACH[m], cross), device_id_type=MESH)

    def reach_back(source, into, sem_out, sem_in, m):
        return pltpu.make_async_remote_copy(
            src_ref=source, dst_ref=into.at[m], send_sem=sem_out.at[m], recv_sem=sem_in.at[m],
            device_id=(wide + REACH[m], cross), device_id_type=MESH)

    def each_reach(make, act):
        for m, by in enumerate(REACH):
            @pl.when(within(wide, by, n_wide))
            def _(m=m):
                act(make(m))

    def sides(s, n):
        if n < 2:
            return send_x.at[s, n], got_x.at[s, n], got_x.at[s, opposite(n)]
        if n < 4:
            return send_y.at[s, n - 2], got_y.at[s, n - 2], got_y.at[s, opposite(n) - 2]
        return send_e.at[s, n - 4], got_e.at[s, n - 4], got_e.at[s, opposite(n) - 4]

    def outgoing(s, n):
        source, _, target = sides(s, n)
        return pltpu.make_async_remote_copy(
            src_ref=source, dst_ref=target, send_sem=send_sem.at[s, n],
            recv_sem=recv_sem.at[s, opposite(n)], device_id=place(n), device_id_type=MESH)

    def incoming(s, n):
        source, target, _ = sides(s, n)
        return pltpu.make_async_remote_copy(
            src_ref=source, dst_ref=target, send_sem=send_sem.at[s, n],
            recv_sem=recv_sem.at[s, n], device_id=place(n), device_id_type=MESH)

    def exchange_start(t, s):
        for n in range(4, 8):
            dx, dy = NEIGHBOURS[n]
            i, j = (4 if dx > 0 else 0), (4 if dy > 0 else 0)
            for c in range(3):
                send_e[s, n - 4, c * 8 : c * 8 + 5] = held[
                    t, pl.ds(c * PER + j * 40 + i, 5, stride=8)]
        for n in (4, 5, 6, 7):
            @pl.when(present(n))
            def _(n=n):
                outgoing(s, n).start()
        for side in range(2):
            send_x[s, side, :75] = held[t, pl.ds(4 * side, 75, stride=8)]
        for n in (0, 1):
            @pl.when(present(n))
            def _(n=n):
                outgoing(s, n).start()
        for side in range(2):
            face = jnp.concatenate(
                [held[t, c * PER + side * 160 : c * PER + side * 160 + 40] for c in range(3)], 0)
            first, second = face[:64], face[64:]
            rolled = pltpu.roll(second, 64, 1)
            use = spread_to(low if side == 0 else ~low, 56)
            send_y[s, side, :56] = jnp.where(use, first[:56], rolled)
            send_y[s, side, 56:] = first[56:]
        for n in (2, 3):
            @pl.when(present(n))
            def _(n=n):
                outgoing(s, n).start()

    def exchange_finish(t, s):
        for n in (2, 3):
            @pl.when(present(n))
            def _(n=n):
                incoming(s, n).wait_recv()
        for side in range(2):
            got = got_y[s, side]
            use = spread_to(low if side == 0 else ~low, 64)
            first = jnp.where(use, pltpu.roll(got, 64, 1), 0.0)
            second = jnp.where(use[:56], got[:56], 0.0)
            more = jnp.concatenate([first, second], 0)
            for c in range(3):
                at = c * PER + side * 160
                held[t, at : at + 40] = held[t, at : at + 40] + more[c * 40 : c * 40 + 40]
        for n in (0, 1):
            @pl.when(present(n))
            def _(n=n):
                incoming(s, n).wait_recv()
        for side in range(2):
            value = held[t, pl.ds(4 * side, 75, stride=8)] + got_x[s, side, :75]
            held[t, pl.ds(4 * side, 75, stride=8)] = value
        for n in (4, 5, 6, 7):
            @pl.when(present(n))
            def _(n=n):
                incoming(s, n).wait_recv()
        for n in range(4, 8):
            dx, dy = NEIGHBOURS[n]
            i, j = (4 if dx > 0 else 0), (4 if dy > 0 else 0)
            use = low if dy < 0 else ~low
            for c in range(3):
                more = jnp.where(use, pltpu.roll(got_e[s, n - 4, c * 8 : c * 8 + 8], 64, 1), 0.0)
                at = pl.ds(c * PER + j * 40 + i, 5, stride=8)
                held[t, at] = held[t, at] + more[:5]
        for n in range(8):
            @pl.when(present(n))
            def _(n=n):
                outgoing(s, n).wait_send()

    fibre = [elem_ref[i : i + 1, :] for i in range(3)]
    slopes = lagrange_slopes(gll_points()[0], gll_points()[0])

    def across(ref, at, table):
        total = None
        for i in range(5):
            row = jnp.broadcast_to(ref[pl.ds(at + i, 1), :], (8, LANES))
            term = column_ref[(table * 5 + i) * 8 : (table * 5 + i) * 8 + 8] * row
            total = term if total is None else total + term
        return total

    def elements(t, into):
        source = held.at[t]
        target = held.at[into]
        for c in range(3):
            for k in range(5):
                at = [c * PER + j * 40 + k * 8 for j in range(5)]
                for j, v in enumerate(along_line([source[a : a + 8] for a in at], slopes)):
                    slope_y[at[j] : at[j] + 8] = v

        def layer(j, carry):
            base = pl.multiple_of(j * 40, 8)

            def at(c, k):
                return pl.ds(pl.multiple_of(base + (c * PER + k * 8), 8), 8)

            grad_z = [along_line([source[at(c, k), :] for k in range(5)], slopes) for c in range(3)]
            flux_z = [[None] * 5 for _ in range(3)]
            for k in range(5):
                g = [
                    [across(source, base + (c * PER + k * 8), 0), slope_y[at(c, k), :], grad_z[c][k]]
                    for c in range(3)
                ]
                part = stresses(g, fibre, mass_w[at(0, k), :])
                for c in range(3):
                    flux_x[at(c, k), :] = part[c, 0]
                    flux_y[at(c, k), :] = part[c, 1]
                    flux_z[c][k] = part[c, 2]
            for c in range(3):
                pull = along_line(flux_z[c], slopes.T)
                for k in range(5):
                    mass = MASS_COEF * weight_ref[at(0, k), :] * source[at(c, k), :]
                    target[at(c, k), :] = (
                        pull[k] + mass + across(flux_x, base + (c * PER + k * 8), 1))
            return carry

        lax.fori_loop(0, 5, layer, 0)
        for c in range(3):
            for k in range(5):
                at = [c * PER + j * 40 + k * 8 for j in range(5)]
                for j, v in enumerate(along_line([flux_y[a : a + 8] for a in at], slopes.T)):
                    target[at[j] : at[j] + 8] = target[at[j] : at[j] + 8] + v

    inner = spread_to(spot > 0, 8)
    outer = spread_to(spot < 63, 8)

    def gather_local(t):
        for c in range(3):
            for j in range(5):
                at = c * PER + j * 40
                first, last = held[t, at : at + 8], held[t, at + 32 : at + 40]
                held[t, at : at + 8] = first + jnp.where(inner, pltpu.roll(last, 1, 1), 0.0)
                held[t, at + 32 : at + 40] = last + jnp.where(outer, pltpu.roll(first, 127, 1), 0.0)
            at = c * PER
            first, last = held[t, at : at + 40], held[t, at + 160 : at + 200]
            use = spread_to(low, 40)
            held[t, at : at + 40] = first + jnp.where(use, 0.0, pltpu.roll(last, 64, 1))
            held[t, at + 160 : at + 200] = spread_to(keep_y, 40) * (
                last + jnp.where(use, pltpu.roll(first, 64, 1), 0.0))
        held[t, pl.ds(4, 75, stride=8)] = held[t, pl.ds(4, 75, stride=8)] * one_x

    def square(t):
        total = jnp.zeros((8, LANES), f32)
        tail = jnp.zeros((8, LANES), f32)
        for c in range(3):
            for j in range(4):
                for k in range(5):
                    at = c * PER + j * 40 + k * 8
                    v = held[t, at : at + 8]
                    if k < 4:
                        total = total + v * v
                    else:
                        tail = tail + v * v
        total = total + jnp.where(ends, tail, 0.0)
        total = jnp.where(sub < 4, total, 0.0)
        return jnp.sum(total, axis=0, keepdims=True)

    def z_sums():
        return [
            z_copy(sums.at[0], got_z.at[k - 1], z_send, z_recv, k) for k in range(1, n_cross)
        ]

    def w_sums(slot):
        return [
            pltpu.make_async_remote_copy(
                src_ref=sums.at[slot], dst_ref=got_w.at[slot - 1, k],
                send_sem=w_send.at[slot - 1, k], recv_sem=w_recv.at[slot - 1, k],
                device_id=peer, device_id_type=MESH)
            for k, peer in enumerate(w_peers)
        ]

    def finish_sums(copies, own, got):
        for copy in copies:
            copy.wait_recv()
        total = own
        for k in range(len(copies)):
            total = total + got[k]
        for copy in copies:
            copy.wait_send()
        return total

    def apply_all(base):
        def step(t, carry):
            elements(t, t + 1)
            gather_local(t + 1)

            @pl.when(t == 0)
            def _():
                held[1] = load[...] - held[1]

            s = lax.rem(t + base, 2)
            exchange_start(t + 1, s)
            exchange_finish(t + 1, s)
            return carry

        lax.fori_loop(0, 4, step, 0)

    exchange_start(0, 0)
    for k in range(1, n_cross):
        z_copy(elem_z.at[cross], elem_z.at[cross], ez_send, ez_recv, k).start()
    unpack(rhs_ref, load)
    exchange_finish(0, 0)
    for k in range(1, n_cross):
        z_copy(elem_z.at[from_z(k)], elem_z.at[from_z(k)], ez_send, ez_recv, k).wait_recv()
    for q in range(4):
        for m in range(4):
            elem_out[m * 4 + q : m * 4 + q + 1] = elem_z[q, m : m + 1]
    for k in range(1, n_cross):
        z_copy(elem_z.at[cross], elem_z.at[cross], ez_send, ez_recv, k).wait_send()
    each_reach(lambda m: reach_out(elem_out, elem_in, er_send, er_recv, m), lambda c: c.start())

    apply_all(1)
    for n in range(4):
        sums[0, n : n + 1] = square(n + 1)
    copies = z_sums()
    for copy in copies:
        copy.start()
    elements(4, 5)
    total = finish_sums(copies, sums[0], got_z)
    sums[1] = total
    copies = w_sums(1)
    for copy in copies:
        copy.start()

    points = gll_points()[0]
    here = jnp.where(sub < 4, 1.0, 0.0)

    def restrict(n, carry):
        last = n == 4
        own_k = jnp.where(ends | last, 1.0, 0.0)
        own_j = jnp.where(last, keep_y, 0.0)
        own_i = here + jnp.where((sub == 4) & last, one_x, 0.0)
        columns = [column_ref[80 + 8 * i2 : 88 + 8 * i2] * own_i for i2 in range(2)]
        for c in range(3):
            lines = []
            for j in range(5):
                u = [held[n + 1, c * PER + j * 40 + k * 8 : c * PER + j * 40 + k * 8 + 8]
                     for k in range(5)]
                first, second = u[0], own_k * u[4]
                for k in range(1, 4):
                    part = float(points[k]) * u[k]
                    first, second = first + (u[k] - part), second + part
                lines.append((first, second))
            for k in range(2):
                first, second = lines[0][k], own_j * lines[4][k]
                for j in range(1, 4):
                    part = float(points[j]) * lines[j][k]
                    first, second = first + (lines[j][k] - part), second + part
                for j2, value in enumerate((first, second)):
                    for i2 in range(2):
                        row = j2 * 12 + i2 * 6 + c * 2 + k
                        rest[cross, n, row : row + 1] = jnp.sum(
                            value * columns[i2], axis=0, keepdims=True)
        return carry

    lax.fori_loop(0, 5, restrict, 0)
    for k in range(1, n_cross):
        z_copy(rest.at[cross], rest.at[cross], cz_send, cz_recv, k).start()

    each_reach(lambda m: reach_back(elem_out, elem_in, er_send, er_recv, m), lambda c: c.wait_recv())
    for m, by in enumerate(REACH):
        if by >= -HOME:
            elem_c[pl.ds(HOME + by, 16, stride=8)] = elem_in[m]
    elem_c[pl.ds(HOME, 16, stride=8)] = elem_out[...]
    for q in range(4):
        at = (12 + q) * 8
        elem_c[at : at + 8] = jnp.where(sub < 7, elem_c[at : at + 8], 0.0)
    each_reach(lambda m: reach_out(elem_out, elem_in, er_send, er_recv, m), lambda c: c.wait_send())

    total = finish_sums(copies, sums[1], got_w.at[0])
    norms = jnp.sum(total, axis=1, keepdims=True)
    largest = jnp.broadcast_to(estimate([norms[n : n + 1] for n in range(4)]), (1, LANES))
    step_poly, rest_poly = smoothing(largest, FINE_RATIO)

    for k in range(1, n_cross):
        z_copy(rest.at[from_z(k)], rest.at[from_z(k)], cz_send, cz_recv, k).wait_recv()
    blocks = []
    for q in range(4):
        value = rest_poly[0] * rest[q, 0]
        for n in range(1, 5):
            value = value + rest_poly[n] * rest[q, n]
        blocks.append(value)
    for k in range(1, n_cross):
        z_copy(rest.at[cross], rest.at[cross], cz_send, cz_recv, k).wait_send()
    nothing = jnp.zeros((12, LANES), f32)
    for q in range(4):
        before = blocks[q - 1][12:24] if q > 0 else nothing
        swapped = pltpu.roll(jnp.where(spread_to(low, 12), blocks[q][12:24], before), 64, 1)
        value = blocks[q][0:12] + swapped
        for i2 in range(2):
            coarse_out[i2 * 24 + q * 6 : i2 * 24 + q * 6 + 6] = value[i2 * 6 : i2 * 6 + 6]
    each_reach(lambda m: reach_out(coarse_out, reach_in, cr_send, cr_recv, m), lambda c: c.start())

    def add_steps(c, carry):
        at = pl.ds(pl.multiple_of(c * PER, 8), PER)
        value = held[0, at]
        for n in range(4):
            value = value + step_poly[n] * held[n + 1, at]
        held[0, at] = value
        return carry

    lax.fori_loop(0, 3, add_steps, 0)
    each_reach(lambda m: reach_back(coarse_out, reach_in, cr_send, cr_recv, m), lambda c: c.wait_recv())

    vertex[0, pl.ds(HOME, 24, stride=8)] = coarse_out[0:24]
    vertex[0, pl.ds(HOME + 1, 24, stride=8)] = coarse_out[24:48]
    for first in (True, False):
        for m, by in enumerate(REACH):
            s = HOME + by if first else HOME + 1 + by
            if 0 <= s < 8:
                part = reach_in[m, 0:24] if first else reach_in[m, 24:48]
                vertex[0, pl.ds(s, 24, stride=8)] = vertex[0, pl.ds(s, 24, stride=8)] + part
    each_reach(lambda m: reach_out(coarse_out, reach_in, cr_send, cr_recv, m), lambda c: c.wait_send())
    free = jnp.where(wide - HOME + sub < n_wide, 1.0, 0.0)

    def close(n, q):
        for c in range(3):
            at = (q * 6 + c * 2) * 8
            first, last = gather[pl.ds(at, 8)], gather[pl.ds(at + 8, 8)]
            first = first + jnp.where(inner, pltpu.roll(last, 1, 1), 0.0)
            vertex[n, pl.ds(at, 8)] = first * free
            vertex[n, pl.ds(at + 8, 8)] = free * jnp.where(outer, pltpu.roll(first, 127, 1), last)

    def close_all(n):
        lax.fori_loop(0, 4, lambda q, carry: (close(n, pl.multiple_of(q, 1)), carry)[1], 0)

    gather[...] = vertex[0]
    close_all(0)

    def coarse_step(n, carry):
        gather[...] = jnp.zeros_like(gather)

        def column(q, inside):
            base = pl.multiple_of(q * 48, 8)

            def at(c, k, up=0):
                return pl.ds(pl.multiple_of(base + (c * 16 + k * 8 + up * 48), 8), 8)

            def data(m):
                return elem_c[pl.ds(pl.multiple_of(m * 32 + q * 8, 8), 8)]

            fib = [data(0), data(1), data(2)]
            stiff = data(3)
            mass = jnp.where(stiff > 0.0, 0.125 * MASS_COEF, 0.0)
            scale = 0.125 * stiff
            grads, values = [], []
            for c in range(3):
                u = [[None, None], [None, None]]
                for k in range(2):
                    w = vertex[n, at(c, k), :]
                    u[0][k] = w
                    u[1][k] = pltpu.roll(jnp.where(low, vertex[n, at(c, k, 1), :], w), 64, 1)
                x = [[to_gauss(u[j][k], pltpu.roll(u[j][k], 7, 0)) for k in range(2)] for j in range(2)]
                gx = [[None, None], [None, None]]
                halves = [to_gauss(x[0][k][2], x[1][k][2]) for k in range(2)]
                for qj in range(2):
                    gx[qj] = to_gauss(halves[0][qj], halves[1][qj])[:2]
                gy, gz = [None, None], [[None, None], [None, None]]
                v = [[[None, None], [None, None]], [[None, None], [None, None]]]
                for qi in range(2):
                    y = [to_gauss(x[0][k][qi], x[1][k][qi]) for k in range(2)]
                    gy[qi] = to_gauss(y[0][2], y[1][2])[:2]
                    for qj in range(2):
                        v[qj][0][qi], v[qj][1][qi], gz[qj][qi] = to_gauss(y[0][qj], y[1][qj])
                grads.append((gx, gy, gz))
                values.append(v)
            part = {}
            for qj in range(2):
                for qk in range(2):
                    for qi in range(2):
                        g = [[gx[qj][qk], gy[qi][qk], gz[qj][qi]] for gx, gy, gz in grads]
                        part[qj, qk, qi] = stresses(g, fib, scale)
            for c in range(3):
                pair = ((0, 0), (0, 1), (1, 0), (1, 1))
                y = {}
                for qj, qi in pair:
                    y[qj, qi] = from_gauss(
                        mass * values[c][qj][0][qi], mass * values[c][qj][1][qi],
                        part[qj, 0, qi][c, 2] + part[qj, 1, qi][c, 2])
                x = {}
                for qi in range(2):
                    tilt = from_gauss(*[
                        part[0, qk, qi][c, 1] + part[1, qk, qi][c, 1] for qk in range(2)])
                    for k in range(2):
                        x[0, k, qi], x[1, k, qi] = from_gauss(y[0, qi][k], y[1, qi][k], tilt[k])
                half = [
                    from_gauss(*[part[qj, qk, 0][c, 0] + part[qj, qk, 1][c, 0] for qk in range(2)])
                    for qj in range(2)
                ]
                for k in range(2):
                    steep = from_gauss(half[0][k], half[1][k])
                    w = []
                    for j in range(2):
                        first, last = from_gauss(x[j, k, 0], x[j, k, 1], steep[j])
                        w.append(first + pltpu.roll(last, 1, 0))
                    other = pltpu.roll(w[1], 64, 1)
                    gather[at(c, k), :] = gather[at(c, k), :] + w[0] + jnp.where(low, 0.0, other)
                    gather[at(c, k, 1), :] = jnp.where(low, other, 0.0)
            return inside

        lax.fori_loop(0, 4, column, 0)
        close_all(n + 1)
        return carry

    lax.fori_loop(0, 3, coarse_step, 0)

    def coarse_square(n):
        total = jnp.zeros((8, LANES), f32)
        tail = jnp.zeros((8, LANES), f32)
        for m in range(12):
            first, last = vertex[n, m * 16 : m * 16 + 8], vertex[n, m * 16 + 8 : m * 16 + 16]
            total = total + first * first
            tail = tail + last * last
        return (total + jnp.where(ends, tail, 0.0))[HOME : HOME + 1]

    for n in range(4):
        sums[2, n : n + 1] = coarse_square(n)
    copies = w_sums(2)
    for copy in copies:
        copy.start()
    total = finish_sums(copies, sums[2], got_w.at[1])
    norms = jnp.sum(total, axis=1, keepdims=True)
    coarse_largest = jnp.broadcast_to(estimate([norms[n : n + 1] for n in range(4)]), (1, LANES))
    coarse_poly, _ = smoothing(coarse_largest, COARSE_RATIO)
    left, right = column_ref[80:88], column_ref[88:96]
    for c in range(3):
        ends_k = []
        for k in range(2):
            w = []
            for up in range(2):
                at = pl.ds(pl.multiple_of((cross + up) * 48, 8) + (c * 16 + k * 8), 8)
                value = coarse_poly[0] * vertex[0, at]
                for n in range(1, 4):
                    value = value + coarse_poly[n] * vertex[n, at]
                w.append(value)
            ends_k.append((w[0], pltpu.roll(jnp.where(low, w[1], w[0]), 64, 1)))
        own = [ends_k[k][0][HOME : HOME + 1] for k in range(2)]
        for ey in range(2):
            a, b = own if ey == 0 else [pltpu.roll(v, 64, 1) for v in own]
            line = jnp.where(low[:1], a, pltpu.roll(b, 1, 1))
            cor_ref[c, 0, ey : ey + 1, :] = line[:, :65]
        nodes = []
        for k in range(2):
            first, last = [
                left * jnp.broadcast_to(v[HOME : HOME + 1], (8, LANES))
                + right * jnp.broadcast_to(v[HOME + 1 : HOME + 2], (8, LANES))
                for v in ends_k[k]
            ]
            step = last - first
            nodes.append(
                [first] + [first + float(points[j]) * step for j in range(1, 4)] + [last])
        for j in range(5):
            first, last = nodes[0][j], nodes[1][j]
            step = last - first
            for k in range(5):
                at = c * PER + j * 40 + k * 8
                more = first if k == 0 else last if k == 4 else first + float(points[k]) * step
                held[0, at : at + 8] = held[0, at : at + 8] + more

    apply_all(1)

    for c in range(3):
        for j in range(4):
            for k in range(5):
                at = c * PER + j * 40 + k * 8
                value = held[0, at : at + 8]
                for n in range(4):
                    value = value + step_poly[n] * held[n + 1, at : at + 8]
                planes[k, pl.ds(c * 32 + j, 4, stride=8)] = value[:4]
                planes[k, pl.ds(c * 32 + 4 + j, 4, stride=8)] = pltpu.roll(value, 64, 1)[:4]
    use = spread_to(low, 96)
    joined = jnp.concatenate(
        [jnp.where(use, planes[k], pltpu.roll(planes[k + 1], 64, 1)) for k in (0, 2)], 1)
    row = lax.broadcasted_iota(jnp.int32, (256, 256), 0)
    z_at = lax.broadcasted_iota(jnp.int32, (256, 256), 1)
    spread = jnp.where(z_at == 4 * lax.rem(row, 64) + row // 64, 1.0, 0.0)
    out_ref[:, :, :, 0:256] = dot(joined, spread).reshape(3, 4, 8, 256)
    out_ref[:, :, :, 256:257] = planes[4][:, 63:64].reshape(3, 4, 8, 1)


def fibre_vectors(index):
    angle = index.astype(jnp.float32) * (2.0 * math.pi / NFIB)
    tilt = 0.4 * jnp.sin(3.0 * angle)
    return jnp.stack(
        [jnp.cos(angle) * jnp.cos(tilt), jnp.sin(angle) * jnp.cos(tilt), jnp.sin(tilt)]
    )


def on_device(rhs, start, stiffness, fibre_index):
    fibre = fibre_vectors(fibre_index).reshape(3, LANES)
    elem = jnp.concatenate([fibre, stiffness.reshape(1, LANES), jnp.zeros((4, LANES))], 0)
    operands = [start, rhs, elem] + tables()
    vmem = pl.BlockSpec(memory_space=pltpu.VMEM)
    f32 = jnp.float32

    def room(*shape):
        return pltpu.VMEM(shape, f32)

    def flags(*shape):
        return pltpu.SemaphoreType.DMA(shape)

    return pl.pallas_call(
        kernel,
        out_shape=(
            jax.ShapeDtypeStruct(rhs.shape, f32),
            jax.ShapeDtypeStruct((3, 1, 2, 65), f32),
        ),
        in_specs=[vmem] * len(operands),
        out_specs=(vmem, vmem),
        scratch_shapes=[
            room(6, ROWS, LANES),
            room(ROWS, LANES),
            room(PER, LANES),
            room(ROWS, LANES),
            room(ROWS, LANES),
            room(ROWS, LANES),
            room(5, 96, LANES),
            room(2, 2, FACE_X, LANES),
            room(2, 2, FACE_Y, LANES),
            room(2, 4, EDGE, LANES),
            room(2, 2, FACE_X, LANES),
            room(2, 2, FACE_Y, LANES),
            room(2, 4, EDGE, LANES),
            room(4, 5, 24, LANES),
            room(48, LANES),
            room(8, 48, LANES),
            room(4, 8, LANES),
            room(16, LANES),
            room(8, 16, LANES),
            room(128, LANES),
            room(4, 240, LANES),
            room(240, LANES),
            room(3, 8, LANES),
            room(3, 8, LANES),
            room(2, 31, 8, LANES),
            flags(2, 8), flags(2, 8),
            flags(3), flags(3),
            flags(2, 31), flags(2, 31),
            flags(3), flags(3),
            flags(3), flags(3),
            flags(8), flags(8),
            flags(8), flags(8),
        ],
        compiler_params=pltpu.CompilerParams(
            collective_id=0, has_side_effects=True, vmem_limit_bytes=32 * 1024 * 1024
        ),
    )(*operands)


def solution(mesh):
    in_specs = (
        P(None, "wide", "cross", None),
        P(None, "wide", "cross", None),
        P("wide", "cross", None),
        P("wide", "cross", None),
    )
    out_specs = (P(None, "wide", "cross", None), P(None, "wide", "cross", None))
    return jax.shard_map(
        on_device, mesh=mesh, in_specs=in_specs, out_specs=out_specs, check_vma=False
    )
```

time: 110 us -> 85.4 us (0.78)
  Pallas kernels: 96.1 us -> 78.6 us
  local copies, waits for them, and re-layouts: 10.7 us -> 5.79 us
  other arithmetic: 1.72 us -> 0.08 us
    pallas_call x1, Pallas kernels: 96.1 us -> 78.6 us  [on_device(): pl.pallas_call(kernel, out_shape=(jax.ShapeDtypeStruct(rhs.shape, f32), j...]
    slice x12 -> x0, local copies, waits for them, and re-layouts: 6.08 us -> none  [the longest x2 3.34 us: to_rows(): field[..., 4::4][..., None]]
    unnamed x23 -> x12, local copies, waits for them, and re-layouts: 0.3 us -> 4.76 us
    reshape x7 -> x0, local copies, waits for them, and re-layouts: 2.78 us -> none  [the longest x2 1.21 us: to_rows(): field[..., :-1].reshape(3, 4, 8, 64, 4)]
where the time goes in v2:
time: 85.4 us; the launch traced here: 85.1 us
  Pallas kernels  78.6 us (92%)
  local copies, waits for them, and re-layouts  5.79 us (7%)
    pallas_call x1, Pallas kernels, on_device(): pl.pallas_call(kernel, out_shape=(jax.ShapeDtypeStruct(rhs.shape, f32), j...  78.6 us
    unnamed x12, local copies, waits for them, and re-layouts  4.76 us

profile of v2, /device:TPU:7, one launch (start us, length us, event | category | flops | bytes accessed | tf_op | source)
XLA Modules:
  0.0 85.1 jit_solution(7317378565939803960)
XLA Ops:
  0.6 0.0 copy-start.4
  0.6 0.8 reshape.14
  1.4 0.0 copy-done.4
  1.4 0.1 fusion
  1.5 0.1 stack.12
  1.6 0.1 stack.11
  1.7 0.1 stack.10
  1.8 0.0 copy-start
  1.8 0.9 %copy-done = f32[3,4,8,257]{3,2,1,0:T(8,128)S(1)} copy-done((f32[3,4,8,257]{3,2,1,0:T(8,128)S(1)}, f32[3,4,8,257]{3,2,1,0:T(8,128)}, u32[]{:S(2)}) %copy-start) | copy-done | bytes 98712
  2.7 0.0 copy-start.1
  2.7 0.9 %copy-done.1 = f32[3,4,8,257]{3,2,1,0:T(8,128)S(1)} copy-done((f32[3,4,8,257]{3,2,1,0:T(8,128)S(1)}, f32[3,4,8,257]{3,2,1,0:T(8,128)}, u32[]{:S(2)}) %copy-start.1) | copy-done | bytes 98712
  3.6 0.0 copy-start.2
  3.6 0.9 %copy-done.2 = f32[200,128]{1,0:T(8,128)S(1)} copy-done((f32[200,128]{1,0:T(8,128)S(1)}, f32[200,128]{1,0:T(8,128)}, u32[]{:S(2)}) %copy-start.2) | copy-done | bytes 102424
  4.5 0.0 copy-start.3
  4.5 0.8 copy-done.3
  5.3 78.6 %shard_map.77 = (f32[3,4,8,257]{3,2,1,0:T(8,128)S(1)}, f32[3,1,2,65]{3,2,1,0:T(2,128)S(1)}) custom-call(f32[3,4,8,257]{3,2,1,0:T(8,128)S(1)} %copy-done, f32[3,4,8,257]{3,2,1,0:T(8,128)S(1)} %copy-done.1, f32[8,128]{1,0:T(8,128)S(1)} %concatenate.5.elem_ref, f32[200,128]{1,0:T(8,128)S(1)} %copy-done.2, f32[96,128]{1,0:T(8,128)S(1)} %copy-done.3), custom_call_target="tpu_custom_call" | custom-call | tf_op jit(solution)/shard_map/pallas_call | solution.py:808
  83.9 0.7 copy.10
  84.5 0.6 copy.11
  (2 shorter events, 0.0 us)
Async XLA Ops:
  0.6 0.8 copy-start.4
  1.8 0.9 %copy-start = (f32[3,4,8,257]{3,2,1,0:T(8,128)S(1)}, f32[3,4,8,257]{3,2,1,0:T(8,128)}, u32[]{:S(2)}) copy-start(f32[3,4,8,257]{3,2,1,0:T(8,128)} %start_ref.1) | copy-start | bytes 296068
  2.7 0.9 %copy-start.1 = (f32[3,4,8,257]{3,2,1,0:T(8,128)S(1)}, f32[3,4,8,257]{3,2,1,0:T(8,128)}, u32[]{:S(2)}) copy-start(f32[3,4,8,257]{3,2,1,0:T(8,128)} %rhs_ref.1) | copy-start | bytes 296068
  3.6 0.9 %copy-start.2 = (f32[200,128]{1,0:T(8,128)S(1)}, f32[200,128]{1,0:T(8,128)}, u32[]{:S(2)}) copy-start(f32[200,128]{1,0:T(8,128)} %constant.13.clone.weight_ref) | copy-start | bytes 307204
  4.5 0.8 copy-start.3

commit v3 on v2

--- a/solution.py
+++ b/solution.py
@@ -26,6 +26,9 @@
 FACE_X, FACE_Y, EDGE = 80, 64, 24
 REACH = (-4, -3, -2, -1, 1, 2, 3, 4)
 HOME = 3
+FAR_FIRST = sorted(range(31), key=lambda k: -min(k + 1, 31 - k))
+TOP_SELF = LAMBDA_COEF + 4.0 * SHEAR_CROSS + (SHEAR_ALONG - SHEAR_CROSS)
+TOP_ALONG = 5.0 * (SHEAR_ALONG - SHEAR_CROSS) + FIBRE_COEF
 
 
 def gll_points():
@@ -63,9 +66,14 @@
     columns[5:10, :5] = slopes[:, :, None]
     columns[10, :5] = (1.0 - points)[:, None]
     columns[11, :5] = points[:, None]
+    columns = columns.reshape(96, LANES)
+    angle = np.arange(NFIB) * (2.0 * math.pi / NFIB)
+    tilt = 0.4 * np.sin(3.0 * angle)
+    fibre = np.zeros((8, LANES))
+    fibre[:3, :NFIB] = [np.cos(angle) * np.cos(tilt), np.sin(angle) * np.cos(tilt), np.sin(tilt)]
     parts = (
         np.broadcast_to(cube.reshape(-1)[:, None], (PER, LANES)),
-        columns.reshape(96, LANES),
+        np.concatenate([columns, fibre], 0),
     )
     return [jnp.asarray(np.ascontiguousarray(part), dtype=jnp.float32) for part in parts]
 
@@ -76,22 +84,15 @@
     )
 
 
-GAUSS = 0.5 / math.sqrt(3.0)
-
-
-def to_gauss(u0, u1):
-    slope = u1 - u0
-    middle = u0 + 0.5 * slope
-    part = GAUSS * slope
-    return middle - part, middle + part, slope
-
-
-def from_gauss(a0, a1, slope=None):
-    both = a0 + a1
-    last = 0.5 * both + GAUSS * (a1 - a0)
-    if slope is not None:
-        last = last + slope
-    return both - last, last
+def selected(values, pick):
+    rows = values.shape[0]
+    high = values.astype(jnp.bfloat16)
+    left = values - high.astype(jnp.float32)
+    middle = left.astype(jnp.bfloat16)
+    low = (left - middle.astype(jnp.float32)).astype(jnp.bfloat16)
+    out = jnp.dot(
+        jnp.concatenate([high, middle, low], 0), pick, preferred_element_type=jnp.float32)
+    return (out[:rows] + out[rows : 2 * rows]) + out[2 * rows :]
 
 
 def along_line(u, table):
@@ -106,26 +107,37 @@
     return [q[0] + p[0], q[1] + p[1], q[2], q[1] - p[1], q[0] - p[0]]
 
 
+def plus(*terms):
+    total = None
+    for term in terms:
+        if term is not None:
+            total = term if total is None else total + term
+    return total
+
+
+def times(a, b):
+    return None if a is None or b is None else a * b
+
+
 def stresses(grad, fibre, scale):
-    shear = {}
+    twice = {}
     for i in range(3):
         for j in range(i, 3):
-            shear[i, j] = grad[i][i] if i == j else 0.5 * (grad[i][j] + grad[j][i])
-            shear[j, i] = shear[i, j]
-    trace = LAMBDA_COEF * (shear[0, 0] + shear[1, 1] + shear[2, 2])
-    along = [
-        shear[i, 0] * fibre[0] + shear[i, 1] * fibre[1] + shear[i, 2] * fibre[2] for i in range(3)
-    ]
-    stretch = fibre[0] * along[0] + fibre[1] * along[1] + fibre[2] * along[2]
-    half = (0.5 * FIBRE_COEF) * stretch
-    cross = 2.0 * (SHEAR_ALONG - SHEAR_CROSS)
+            twice[i, j] = twice[j, i] = (
+                times(grad[i][i], 2.0) if i == j else plus(grad[i][j], grad[j][i]))
+    trace = times(plus(grad[0][0], grad[1][1], grad[2][2]), LAMBDA_COEF)
+    along = [plus(*[times(twice[i, j], fibre[j]) for j in range(3)]) for i in range(3)]
+    stretch = plus(*[times(along[i], fibre[i]) for i in range(3)])
+    half = (0.25 * FIBRE_COEF) * stretch
+    cross = SHEAR_ALONG - SHEAR_CROSS
     pull = [cross * along[i] + half * fibre[i] for i in range(3)]
     out = {}
     for i in range(3):
         for j in range(i, 3):
-            value = 2.0 * SHEAR_CROSS * shear[i, j] + (fibre[i] * pull[j] + pull[i] * fibre[j])
-            if i == j:
-                value = value + trace
+            value = plus(
+                times(twice[i, j], SHEAR_CROSS) if SHEAR_CROSS != 1.0 else twice[i, j],
+                fibre[i] * pull[j] + pull[i] * fibre[j] if i != j else (2.0 * fibre[i]) * pull[i],
+                trace if i == j else None)
             out[i, j] = out[j, i] = value * scale
     return out
 
@@ -166,14 +178,15 @@
 
 
 def kernel(
-    start_ref, rhs_ref, elem_ref, weight_ref, column_ref,
-    out_ref, cor_ref,
+    start_hbm, rhs_hbm, stiff_hbm, index_hbm, weight_hbm, column_hbm,
+    out_ref, last_ref, cor_ref,
+    start_ref, rhs_ref, stiff_ref, index_ref, weight_ref, column_ref, elem_ref,
     held, load, mass_w, slope_y, flux_x, flux_y, planes,
     send_x, send_y, send_e, got_x, got_y, got_e,
-    rest, coarse_out, reach_in, elem_z, elem_out, elem_in, elem_c, vertex, gather,
-    sums, got_z, got_w,
+    rest, coarse_out, tails, tail_in, reach_in, elem_z, elem_out, elem_in, elem_c, vertex, gather,
+    sums, norms, got_z, got_w,
     send_sem, recv_sem, z_send, z_recv, w_send, w_recv, ez_send, ez_recv, cz_send, cz_recv,
-    er_send, er_recv, cr_send, cr_recv,
+    er_send, er_recv, cr_send, cr_recv, in_sem, greeting,
 ):
     wide, cross = lax.axis_index("wide"), lax.axis_index("cross")
     n_wide, n_cross = lax.axis_size("wide"), lax.axis_size("cross")
@@ -202,16 +215,25 @@
     z_peers = [(wide, lax.rem(cross + k, n_cross)) for k in range(1, n_cross)]
     w_peers = [(lax.rem(wide + k, n_wide), cross) for k in range(1, n_wide)]
 
+    loads = [
+        pltpu.make_async_copy(source, target, in_sem.at[n])
+        for n, (source, target) in enumerate((
+            (start_hbm, start_ref), (stiff_hbm, stiff_ref), (index_hbm, index_ref),
+            (column_hbm, column_ref), (weight_hbm, weight_ref), (rhs_hbm, rhs_ref)))
+    ]
+    for copy in loads:
+        copy.start()
+
     got_x[...] = jnp.zeros_like(got_x)
     got_y[...] = jnp.zeros_like(got_y)
     got_e[...] = jnp.zeros_like(got_e)
     reach_in[...] = jnp.zeros_like(reach_in)
     elem_in[...] = jnp.zeros_like(elem_in)
+    got_z[...] = jnp.zeros_like(got_z)
+    got_w[...] = jnp.zeros_like(got_w)
     barrier = pltpu.get_barrier_semaphore()
-    expected = jnp.int32(len(z_peers) + len(w_peers))
-    for peer in z_peers + w_peers:
-        pl.semaphore_signal(barrier, inc=1, device_id=peer, device_id_type=MESH)
-    for n in range(4, 8):
+    expected = jnp.int32(0)
+    for n in (4, 5, 6, 7, 0, 1, 2, 3):
         @pl.when(present(n))
         def _(n=n):
             pl.semaphore_signal(barrier, inc=1, device_id=place(n), device_id_type=MESH)
@@ -232,17 +254,17 @@
     send_x[...] = jnp.zeros_like(send_x)
     send_e[...] = jnp.zeros_like(send_e)
     sums[...] = jnp.zeros_like(sums)
+    norms[...] = jnp.zeros_like(norms)
     vertex[...] = jnp.zeros_like(vertex)
     gather[...] = jnp.zeros_like(gather)
-    mass_w[...] = weight_ref[...] * elem_ref[3:4, :]
-    elem_z[cross] = elem_ref[...]
-
+    tail_in[...] = jnp.zeros_like(tail_in)
+    coarse_out[...] = jnp.zeros_like(coarse_out)
     z_at = lax.broadcasted_iota(jnp.int32, (256, 5 * LANES), 0)
     col = lax.broadcasted_iota(jnp.int32, (256, 5 * LANES), 1)
-    pick = jnp.where(z_at == 4 * lax.rem(col, 64) + col // LANES, 1.0, 0.0)
+    pick = jnp.where(z_at == 4 * lax.rem(col, 64) + col // LANES, 1.0, 0.0).astype(jnp.bfloat16)
 
     def unpack(ref, into):
-        nodes = dot(ref[:, :, :, 0:256].reshape(96, 256), pick)
+        nodes = selected(ref[:, :, :, 0:256].reshape(96, 256), pick)
         final = jnp.broadcast_to(ref[:, :, :, 256:257].reshape(96, 1), (96, LANES))
         for k in range(5):
             part = nodes[:, k * LANES : k * LANES + LANES]
@@ -259,7 +281,18 @@
                     at = c * PER + j * 40 + k * 8
                     into[at : at + 4] = jnp.where(low[:4], first, second)
 
+    loads[0].wait()
     unpack(start_ref, held.at[0])
+    for copy in loads[1:5]:
+        copy.wait()
+    index = lax.broadcasted_iota(jnp.int32, (64, 64), 0)
+    chosen = jnp.concatenate(
+        [jnp.where(index_ref[0, n : n + 1, :] == index, 1.0, 0.0) for n in range(2)], 1)
+    elem_ref[...] = dot(column_ref[96:104, :64], chosen)
+    elem_ref[3:4, :] = jnp.concatenate([stiff_ref[0, n : n + 1, :] for n in range(2)], 1)
+    mass_w[...] = weight_ref[...] * elem_ref[3:4, :]
+    weight_ref[...] = MASS_COEF * weight_ref[...]
+    elem_z[cross] = elem_ref[...]
     pl.semaphore_wait(barrier, expected)
 
     def z_copy(source, target, sem_out, sem_in, k, back=False):
@@ -415,7 +448,7 @@
             for c in range(3):
                 pull = along_line(flux_z[c], slopes.T)
                 for k in range(5):
-                    mass = MASS_COEF * weight_ref[at(0, k), :] * source[at(c, k), :]
+                    mass = weight_ref[at(0, k), :] * source[at(c, k), :]
                     target[at(c, k), :] = (
                         pull[k] + mass + across(flux_x, base + (c * PER + k * 8), 1))
             return carry
@@ -463,29 +496,56 @@
 
     def z_sums():
         return [
-            z_copy(sums.at[0], got_z.at[k - 1], z_send, z_recv, k) for k in range(1, n_cross)
+            z_copy(sums.at[0, 0:1], got_z.at[k - 1 : k], z_send, z_recv, k)
+            for k in range(1, n_cross)
         ]
 
     def w_sums(slot):
         return [
             pltpu.make_async_remote_copy(
-                src_ref=sums.at[slot], dst_ref=got_w.at[slot - 1, k],
+                src_ref=sums.at[slot, 0:1], dst_ref=got_w.at[slot - 1, k : k + 1],
                 send_sem=w_send.at[slot - 1, k], recv_sem=w_recv.at[slot - 1, k],
-                device_id=peer, device_id_type=MESH)
-            for k, peer in enumerate(w_peers)
+                device_id=w_peers[k], device_id_type=MESH)
+            for k in FAR_FIRST
         ]
 
     def finish_sums(copies, own, got):
         for copy in copies:
             copy.wait_recv()
-        total = own
-        for k in range(len(copies)):
-            total = total + got[k]
+        total = own + jnp.sum(got[...], axis=0, keepdims=True)
         for copy in copies:
             copy.wait_send()
         return total
 
-    def apply_all(base):
+    def in_one_row(parts):
+        whole = jnp.sum(parts, axis=1, keepdims=True)
+        return jnp.sum(jnp.where(lane // 32 == sub, whole, 0.0), axis=0, keepdims=True)
+
+    def out_of_row(row):
+        whole = jnp.sum(jnp.where(lane == 32 * sub, row, 0.0), axis=1, keepdims=True)
+        return [jnp.broadcast_to(whole[n : n + 1], (1, LANES)) for n in range(4)]
+
+    def greet(t):
+        for stage in range(5):
+            @pl.when(t == stage)
+            def _(stage=stage):
+                for side in range(2):
+                    sign = (-1, 1)[side]
+                    if stage > 0:
+                        @pl.when(within(wide, sign * 2**stage, n_wide))
+                        def _(side=side):
+                            pl.semaphore_wait(greeting.at[stage - 1, side], 1)
+                if stage < 4:
+                    for side in range(2):
+                        by = (-1, 1)[side] * 2 ** (stage + 1)
+
+                        @pl.when(within(wide, by, n_wide))
+                        def _(side=side, by=by):
+                            pl.semaphore_signal(
+                                greeting.at[stage, 1 - side], inc=1, device_id=(wide + by, cross),
+                                device_id_type=MESH)
+
+    def apply_all(base, squares, late=None):
         def step(t, carry):
             elements(t, t + 1)
             gather_local(t + 1)
@@ -496,16 +556,36 @@
 
             s = lax.rem(t + base, 2)
             exchange_start(t + 1, s)
+            if squares:
+                greet(t)
+                norms[pl.ds(t, 1)] = square(t)
+            if late is not None:
+                @pl.when(t == 3)
+                def _():
+                    late()
             exchange_finish(t + 1, s)
             return carry
 
         lax.fori_loop(0, 4, step, 0)
 
     exchange_start(0, 0)
+    loads[5].wait()
+    unpack(rhs_ref, load)
+    exchange_finish(0, 0)
+    apply_all(1, True)
+    norms[4:5] = square(4)
+    sums[0, 0:1] = in_one_row(norms[1:9])
+    copies = z_sums()
+    for copy in copies:
+        copy.start()
     for k in range(1, n_cross):
         z_copy(elem_z.at[cross], elem_z.at[cross], ez_send, ez_recv, k).start()
-    unpack(rhs_ref, load)
-    exchange_finish(0, 0)
+    greet(4)
+    elements(4, 5)
+    sums[1, 0:1] = finish_sums(copies, sums[0, 0:1], got_z)
+    copies = w_sums(1)
+    for copy in copies:
+        copy.start()
     for k in range(1, n_cross):
         z_copy(elem_z.at[from_z(k)], elem_z.at[from_z(k)], ez_send, ez_recv, k).wait_recv()
     for q in range(4):
@@ -514,19 +594,6 @@
     for k in range(1, n_cross):
         z_copy(elem_z.at[cross], elem_z.at[cross], ez_send, ez_recv, k).wait_send()
     each_reach(lambda m: reach_out(elem_out, elem_in, er_send, er_recv, m), lambda c: c.start())
-
-    apply_all(1)
-    for n in range(4):
-        sums[0, n : n + 1] = square(n + 1)
-    copies = z_sums()
-    for copy in copies:
-        copy.start()
-    elements(4, 5)
-    total = finish_sums(copies, sums[0], got_z)
-    sums[1] = total
-    copies = w_sums(1)
-    for copy in copies:
-        copy.start()
 
     points = gll_points()[0]
     here = jnp.where(sub < 4, 1.0, 0.0)
@@ -573,9 +640,7 @@
         elem_c[at : at + 8] = jnp.where(sub < 7, elem_c[at : at + 8], 0.0)
     each_reach(lambda m: reach_out(elem_out, elem_in, er_send, er_recv, m), lambda c: c.wait_send())
 
-    total = finish_sums(copies, sums[1], got_w.at[0])
-    norms = jnp.sum(total, axis=1, keepdims=True)
-    largest = jnp.broadcast_to(estimate([norms[n : n + 1] for n in range(4)]), (1, LANES))
+    largest = estimate(out_of_row(finish_sums(copies, sums[1, 0:1], got_w.at[0])))
     step_poly, rest_poly = smoothing(largest, FINE_RATIO)
 
     for k in range(1, n_cross):
@@ -593,8 +658,17 @@
         before = blocks[q - 1][12:24] if q > 0 else nothing
         swapped = pltpu.roll(jnp.where(spread_to(low, 12), blocks[q][12:24], before), 64, 1)
         value = blocks[q][0:12] + swapped
+        moved = pltpu.roll(value, 1, 1)
         for i2 in range(2):
-            coarse_out[i2 * 24 + q * 6 : i2 * 24 + q * 6 + 6] = value[i2 * 6 : i2 * 6 + 6]
+            for c in range(3):
+                first, last = i2 * 6 + c * 2, i2 * 6 + c * 2 + 1
+                row = i2 * 12 + q * 3 + c
+                coarse_out[row : row + 1] = value[first : first + 1] + jnp.where(
+                    inner[:1], moved[last : last + 1], 0.0)
+                tails[row : row + 1] = value[last : last + 1]
+    late = pltpu.roll(
+        jnp.where(spread_to(ends, 24), tails[...], 0.0), 1, 1, stride=1, stride_axis=0)
+    coarse_out[24:25] = jnp.sum(late, axis=0, keepdims=True)
     each_reach(lambda m: reach_out(coarse_out, reach_in, cr_send, cr_recv, m), lambda c: c.start())
 
     def add_steps(c, carry):
@@ -608,16 +682,21 @@
     lax.fori_loop(0, 3, add_steps, 0)
     each_reach(lambda m: reach_back(coarse_out, reach_in, cr_send, cr_recv, m), lambda c: c.wait_recv())
 
-    vertex[0, pl.ds(HOME, 24, stride=8)] = coarse_out[0:24]
-    vertex[0, pl.ds(HOME + 1, 24, stride=8)] = coarse_out[24:48]
-    for first in (True, False):
-        for m, by in enumerate(REACH):
-            s = HOME + by if first else HOME + 1 + by
+    free = jnp.where(wide - HOME + sub < n_wide, 1.0, 0.0)
+    for i2 in range(2):
+        for by in (0,) + REACH:
+            s = HOME + by + i2
             if 0 <= s < 8:
-                part = reach_in[m, 0:24] if first else reach_in[m, 24:48]
-                vertex[0, pl.ds(s, 24, stride=8)] = vertex[0, pl.ds(s, 24, stride=8)] + part
+                part = coarse_out if by == 0 else reach_in.at[REACH.index(by)]
+                gather[pl.ds(i2 * 96 + s, 12, stride=8)] = part[i2 * 12 : i2 * 12 + 12]
+                tail_in[i2 * 8 + s : i2 * 8 + s + 1] = part[24:25]
+    for m in range(12):
+        first = gather[m * 8 : m * 8 + 8] + gather[96 + m * 8 : 104 + m * 8]
+        last = pltpu.roll(tail_in[0:8], 127 - m, 1) + pltpu.roll(tail_in[8:16], 115 - m, 1)
+        vertex[0, m * 16 : m * 16 + 8] = first * free
+        vertex[0, m * 16 + 8 : m * 16 + 16] = free * jnp.where(
+            outer, pltpu.roll(first, 127, 1), last)
     each_reach(lambda m: reach_out(coarse_out, reach_in, cr_send, cr_recv, m), lambda c: c.wait_send())
-    free = jnp.where(wide - HOME + sub < n_wide, 1.0, 0.0)
 
     def close(n, q):
         for c in range(3):
@@ -628,83 +707,79 @@
             vertex[n, pl.ds(at + 8, 8)] = free * jnp.where(outer, pltpu.roll(first, 127, 1), last)
 
     def close_all(n):
-        lax.fori_loop(0, 4, lambda q, carry: (close(n, pl.multiple_of(q, 1)), carry)[1], 0)
-
-    gather[...] = vertex[0]
-    close_all(0)
+        for q in range(4):
+            close(n, q)
 
     def coarse_step(n, carry):
-        gather[...] = jnp.zeros_like(gather)
-
-        def column(q, inside):
-            base = pl.multiple_of(q * 48, 8)
-
+        carried = {}
+
+        def column(q):
             def at(c, k, up=0):
-                return pl.ds(pl.multiple_of(base + (c * 16 + k * 8 + up * 48), 8), 8)
+                return pl.ds((q + up) * 48 + c * 16 + k * 8, 8)
 
             def data(m):
-                return elem_c[pl.ds(pl.multiple_of(m * 32 + q * 8, 8), 8)]
+                return elem_c[m * 32 + q * 8 : m * 32 + q * 8 + 8]
 
             fib = [data(0), data(1), data(2)]
             stiff = data(3)
-            mass = jnp.where(stiff > 0.0, 0.125 * MASS_COEF, 0.0)
-            scale = 0.125 * stiff
-            grads, values = [], []
+            mass = jnp.where(stiff > 0.0, MASS_COEF, 0.0)
+            modes = []
             for c in range(3):
-                u = [[None, None], [None, None]]
+                m = {}
                 for k in range(2):
                     w = vertex[n, at(c, k), :]
-                    u[0][k] = w
-                    u[1][k] = pltpu.roll(jnp.where(low, vertex[n, at(c, k, 1), :], w), 64, 1)
-                x = [[to_gauss(u[j][k], pltpu.roll(u[j][k], 7, 0)) for k in range(2)] for j in range(2)]
-                gx = [[None, None], [None, None]]
-                halves = [to_gauss(x[0][k][2], x[1][k][2]) for k in range(2)]
-                for qj in range(2):
-                    gx[qj] = to_gauss(halves[0][qj], halves[1][qj])[:2]
-                gy, gz = [None, None], [[None, None], [None, None]]
-                v = [[[None, None], [None, None]], [[None, None], [None, None]]]
-                for qi in range(2):
-                    y = [to_gauss(x[0][k][qi], x[1][k][qi]) for k in range(2)]
-                    gy[qi] = to_gauss(y[0][2], y[1][2])[:2]
-                    for qj in range(2):
-                        v[qj][0][qi], v[qj][1][qi], gz[qj][qi] = to_gauss(y[0][qj], y[1][qj])
-                grads.append((gx, gy, gz))
-                values.append(v)
-            part = {}
-            for qj in range(2):
-                for qk in range(2):
-                    for qi in range(2):
-                        g = [[gx[qj][qk], gy[qi][qk], gz[qj][qi]] for gx, gy, gz in grads]
-                        part[qj, qk, qi] = stresses(g, fib, scale)
+                    beside = pltpu.roll(jnp.where(low, vertex[n, at(c, k, 1), :], w), 64, 1)
+                    for b, v in enumerate((w + beside, beside - w)):
+                        after = pltpu.roll(v, 7, 0)
+                        m[0, b, k], m[1, b, k] = v + after, after - v
+                modes.append({})
+                for a in range(2):
+                    for b in range(2):
+                        first, last = m[a, b, 0], m[a, b, 1]
+                        modes[c][a, b, 0], modes[c][a, b, 1] = first + last, last - first
+            back = [{}, {}, {}]
+
+            def put(c, mode, value):
+                back[c][mode] = back[c][mode] + value if mode in back[c] else value
+
+            for ones, weight in (((0, 0, 0), 16.0), ((1, 0, 0), 48.0), ((0, 1, 0), 48.0), ((0, 0, 1), 48.0)):
+                at_mode = {
+                    d: tuple(1 if d == e else ones[e] for e in range(3))
+                    for d in range(3) if not ones[d]
+                }
+                grad = [
+                    [modes[c][at_mode[d]] if d in at_mode else None for d in range(3)]
+                    for c in range(3)
+                ]
+                part = stresses(grad, fib, stiff * (1.0 / weight))
+                for d in at_mode:
+                    for c in range(3):
+                        put(c, at_mode[d], part[c, d])
+            top = [modes[c][1, 1, 1] for c in range(3)]
+            along = fib[0] * top[0] + fib[1] * top[1] + fib[2] * top[2]
+            along = (stiff * (TOP_ALONG / 144.0)) * along
+            top_scale = stiff * (TOP_SELF / 144.0)
             for c in range(3):
-                pair = ((0, 0), (0, 1), (1, 0), (1, 1))
-                y = {}
-                for qj, qi in pair:
-                    y[qj, qi] = from_gauss(
-                        mass * values[c][qj][0][qi], mass * values[c][qj][1][qi],
-                        part[qj, 0, qi][c, 2] + part[qj, 1, qi][c, 2])
-                x = {}
-                for qi in range(2):
-                    tilt = from_gauss(*[
-                        part[0, qk, qi][c, 1] + part[1, qk, qi][c, 1] for qk in range(2)])
-                    for k in range(2):
-                        x[0, k, qi], x[1, k, qi] = from_gauss(y[0, qi][k], y[1, qi][k], tilt[k])
-                half = [
-                    from_gauss(*[part[qj, qk, 0][c, 0] + part[qj, qk, 1][c, 0] for qk in range(2)])
-                    for qj in range(2)
-                ]
+                put(c, (1, 1, 1), top_scale * top[c] + along * fib[c])
+                for mode, value in modes[c].items():
+                    count = sum(mode)
+                    put(c, mode, (mass * (0.25 ** (3 - count) / 12.0**count)) * value)
                 for k in range(2):
-                    steep = from_gauss(half[0][k], half[1][k])
                     w = []
-                    for j in range(2):
-                        first, last = from_gauss(x[j, k, 0], x[j, k, 1], steep[j])
-                        w.append(first + pltpu.roll(last, 1, 0))
-                    other = pltpu.roll(w[1], 64, 1)
-                    gather[at(c, k), :] = gather[at(c, k), :] + w[0] + jnp.where(low, 0.0, other)
-                    gather[at(c, k, 1), :] = jnp.where(low, other, 0.0)
-            return inside
-
-        lax.fori_loop(0, 4, column, 0)
+                    xs = {}
+                    for a in range(2):
+                        for b in range(2):
+                            first, last = back[c][a, b, 0], back[c][a, b, 1]
+                            xs[a, b] = first + last if k else first - last
+                    for b in range(2):
+                        w.append((xs[0, b] - xs[1, b]) + pltpu.roll(xs[0, b] + xs[1, b], 1, 0))
+                    other = pltpu.roll(w[0] + w[1], 64, 1)
+                    own = jnp.where(low, carried[c, k], other) if q else jnp.where(low, 0.0, other)
+                    gather[at(c, k), :] = (w[0] - w[1]) + own
+                    carried[c, k] = other
+
+        for q in range(4):
+            column(q)
         close_all(n + 1)
         return carry
 
@@ -720,13 +795,12 @@
         return (total + jnp.where(ends, tail, 0.0))[HOME : HOME + 1]
 
     for n in range(4):
-        sums[2, n : n + 1] = coarse_square(n)
+        norms[n : n + 1] = coarse_square(n)
+    sums[2, 0:1] = in_one_row(norms[0:8])
     copies = w_sums(2)
     for copy in copies:
         copy.start()
-    total = finish_sums(copies, sums[2], got_w.at[1])
-    norms = jnp.sum(total, axis=1, keepdims=True)
-    coarse_largest = jnp.broadcast_to(estimate([norms[n : n + 1] for n in range(4)]), (1, LANES))
+    coarse_largest = estimate(out_of_row(finish_sums(copies, sums[2, 0:1], got_w.at[1])))
     coarse_poly, _ = smoothing(coarse_largest, COARSE_RATIO)
     left, right = column_ref[80:88], column_ref[88:96]
     for c in range(3):
@@ -763,39 +837,35 @@
                 more = first if k == 0 else last if k == 4 else first + float(points[k]) * step
                 held[0, at : at + 8] = held[0, at : at + 8] + more
 
-    apply_all(1)
-
-    for c in range(3):
-        for j in range(4):
-            for k in range(5):
-                at = c * PER + j * 40 + k * 8
-                value = held[0, at : at + 8]
-                for n in range(4):
-                    value = value + step_poly[n] * held[n + 1, at : at + 8]
-                planes[k, pl.ds(c * 32 + j, 4, stride=8)] = value[:4]
-                planes[k, pl.ds(c * 32 + 4 + j, 4, stride=8)] = pltpu.roll(value, 64, 1)[:4]
-    use = spread_to(low, 96)
-    joined = jnp.concatenate(
-        [jnp.where(use, planes[k], pltpu.roll(planes[k + 1], 64, 1)) for k in (0, 2)], 1)
     row = lax.broadcasted_iota(jnp.int32, (256, 256), 0)
     z_at = lax.broadcasted_iota(jnp.int32, (256, 256), 1)
-    spread = jnp.where(z_at == 4 * lax.rem(row, 64) + row // 64, 1.0, 0.0)
-    out_ref[:, :, :, 0:256] = dot(joined, spread).reshape(3, 4, 8, 256)
-    out_ref[:, :, :, 256:257] = planes[4][:, 63:64].reshape(3, 4, 8, 1)
-
-
-def fibre_vectors(index):
-    angle = index.astype(jnp.float32) * (2.0 * math.pi / NFIB)
-    tilt = 0.4 * jnp.sin(3.0 * angle)
-    return jnp.stack(
-        [jnp.cos(angle) * jnp.cos(tilt), jnp.sin(angle) * jnp.cos(tilt), jnp.sin(tilt)]
-    )
+    spread = jnp.where(z_at == 4 * lax.rem(row, 64) + row // 64, 1.0, 0.0).astype(jnp.bfloat16)
+
+    def to_nodes(value_at, ref):
+        for c in range(3):
+            for j in range(4):
+                for k in range(5):
+                    value = value_at(pl.ds(c * PER + j * 40 + k * 8, 8))
+                    planes[k, pl.ds(c * 32 + j, 4, stride=8)] = value[:4]
+                    planes[k, pl.ds(c * 32 + 4 + j, 4, stride=8)] = pltpu.roll(value, 64, 1)[:4]
+        use = spread_to(low, 96)
+        joined = jnp.concatenate(
+            [jnp.where(use, planes[k], pltpu.roll(planes[k + 1], 64, 1)) for k in (0, 2)], 1)
+        ref[:, :, :, 0:256] = selected(joined, spread).reshape(3, 4, 8, 256)
+        ref[:, :, :, 256:257] = planes[4][:, 63:64].reshape(3, 4, 8, 1)
+
+    def most(at):
+        value = held[0, at]
+        for n in range(3):
+            value = value + step_poly[n] * held[n + 1, at]
+        return value
+
+    apply_all(1, False, lambda: to_nodes(most, out_ref))
+    to_nodes(lambda at: step_poly[3] * held[4, at], last_ref)
 
 
 def on_device(rhs, start, stiffness, fibre_index):
-    fibre = fibre_vectors(fibre_index).reshape(3, LANES)
-    elem = jnp.concatenate([fibre, stiffness.reshape(1, LANES), jnp.zeros((4, LANES))], 0)
-    operands = [start, rhs, elem] + tables()
+    operands = [start, rhs, stiffness, fibre_index] + tables()
     vmem = pl.BlockSpec(memory_space=pltpu.VMEM)
     f32 = jnp.float32
 
@@ -805,15 +875,23 @@
     def flags(*shape):
         return pltpu.SemaphoreType.DMA(shape)
 
-    return pl.pallas_call(
+    most, last, correction = pl.pallas_call(
         kernel,
         out_shape=(
             jax.ShapeDtypeStruct(rhs.shape, f32),
+            jax.ShapeDtypeStruct(rhs.shape, f32),
             jax.ShapeDtypeStruct((3, 1, 2, 65), f32),
         ),
-        in_specs=[vmem] * len(operands),
-        out_specs=(vmem, vmem),
+        in_specs=[pl.BlockSpec(memory_space=pltpu.HBM)] * len(operands),
+        out_specs=(vmem, vmem, vmem),
         scratch_shapes=[
+            room(3, 4, 8, 257),
+            room(3, 4, 8, 257),
+            room(1, 2, 64),
+            pltpu.VMEM((1, 2, 64), jnp.int32),
+            room(PER, LANES),
+            room(104, LANES),
+            room(8, LANES),
             room(6, ROWS, LANES),
             room(ROWS, LANES),
             room(PER, LANES),
@@ -828,8 +906,10 @@
             room(2, 2, FACE_Y, LANES),
             room(2, 4, EDGE, LANES),
             room(4, 5, 24, LANES),
-            room(48, LANES),
-            room(8, 48, LANES),
+            room(32, LANES),
+            room(24, LANES),
+            room(16, LANES),
+            room(8, 32, LANES),
             room(4, 8, LANES),
             room(16, LANES),
             room(8, 16, LANES),
@@ -837,8 +917,9 @@
             room(4, 240, LANES),
             room(240, LANES),
             room(3, 8, LANES),
-            room(3, 8, LANES),
-            room(2, 31, 8, LANES),
+            room(16, LANES),
+            room(8, LANES),
+            room(2, 32, LANES),
             flags(2, 8), flags(2, 8),
             flags(3), flags(3),
             flags(2, 31), flags(2, 31),
@@ -846,11 +927,14 @@
             flags(3), flags(3),
             flags(8), flags(8),
             flags(8), flags(8),
+            flags(6),
+            pltpu.SemaphoreType.REGULAR((4, 2)),
         ],
         compiler_params=pltpu.CompilerParams(
-            collective_id=0, has_side_effects=True, vmem_limit_bytes=32 * 1024 * 1024
+            collective_id=0, has_side_effects=True, vmem_limit_bytes=60 * 1024 * 1024
         ),
     )(*operands)
+    return most + last, correction
 
 
 def solution(mesh):

time: 85.4 us -> 74.3 us (0.87)
  Pallas kernels: 78.6 us -> 71.3 us
  local copies, waits for them, and re-layouts: 5.79 us -> 0.58 us
  other arithmetic: 0.08 us -> 1.66 us
    pallas_call x1, Pallas kernels: 78.6 us -> 71.3 us  [on_device(): pl.pallas_call(kernel, out_shape=(jax.ShapeDtypeStruct(rhs.shape, f32), j...]
    unnamed x12 -> x3, local copies, waits for them, and re-layouts: 4.76 us -> 0.58 us
    add x0 -> x1, other arithmetic: none -> 1.66 us  [on_device(): return (most + last, correction)]
where the time goes in v3:
time: 74.3 us; the launch traced here: 74.2 us
  Pallas kernels  71.3 us (96%)
  other arithmetic  1.66 us (2%)
    pallas_call x1, Pallas kernels, on_device(): pl.pallas_call(kernel, out_shape=(jax.ShapeDtypeStruct(rhs.shape, f32), j...  71.3 us
    add x1, other arithmetic, on_device(): return (most + last, correction)  1.66 us

profile of v3, /device:TPU:7, one launch (start us, length us, event | category | flops | bytes accessed | tf_op | source)
XLA Modules:
  0.0 74.2 jit_solution(4450477549985728621)
XLA Ops:
  0.6 71.3 %shard_map.77 = (f32[3,4,8,257]{3,2,1,0:T(8,128)}, f32[3,4,8,257]{3,2,1,0:T(8,128)}, f32[3,1,2,65]{3,2,1,0:T(2,128)}) custom-call(f32[3,4,8,257]{3,2,1,0:T(8,128)} %start_hbm.1, f32[3,4,8,257]{3,2,1,0:T(8,128)} %rhs_hbm.1, f32[1,2,64]{2,1,0:T(2,128)} %stiff_hbm.1, s32[1,2,64]{2,1,0:T(2,128)} %index_hbm.1, f32[200,128]{1,0:T(8,128)} %constant.4.clone.weight_hbm, ...), custom_call_target="tpu_custom_call" | custom-call | tf_op jit(solution)/shard_map/pallas_call | solution.py:878
  71.9 0.0 copy-start
  71.9 1.7 %add.3 = f32[3,4,8,257]{3,2,1,0:T(8,128)} add(f32[3,4,8,257]{3,2,1,0:T(8,128)} %get-tuple-element.5, f32[3,4,8,257]{3,2,1,0:T(8,128)} %get-tuple-element.6) | non-fusion elementwise | flops 24672 | bytes 296064 | tf_op jit(solution)/shard_map/add | solution.py:937
  73.6 0.0 copy-done
  73.6 0.6 copy.9
Async XLA Ops:
  71.9 1.7 %copy-start = (f32[3,1,2,65]{3,2,1,0:T(2,128)S(1)}, f32[3,1,2,65]{3,2,1,0:T(2,128)}, u32[]{:S(2)}) copy-start(f32[3,1,2,65]{3,2,1,0:T(2,128)} %get-tuple-element.11) | copy-start | bytes 4684

commit v4 on v3

--- a/solution.py
+++ b/solution.py
@@ -143,38 +143,34 @@
 
 
 def estimate(n):
-    scale = 1.0 / jnp.sqrt(n[0] + 1e-6)
-    last = None
-    for k in range(1, 4):
-        last = jnp.sqrt((n[k] * scale) * scale + 1e-6)
-        scale = scale / last
-    return last
+    scale = 1.0 / (n[0] + 1e-6)
+    for k in range(1, 3):
+        scale = scale / (n[k] * scale + 1e-6)
+    return jnp.sqrt(n[3] * scale + 1e-6)
 
 
 def smoothing(largest, ratio):
-    upper = 1.1 * largest
+    upper = 1.1
     lower = upper / ratio
-    centre = 0.5 * (upper + lower)
-    radius = 0.5 * (upper - lower)
+    centre, radius = 0.5 * (upper + lower), 0.5 * (upper - lower)
     spread = centre / radius
     weight = 1.0 / spread
-    step = [1.0 / centre]
-    rest = [jnp.ones_like(largest)]
-    total = [jnp.zeros_like(largest)] * 4
-
-    def entry(poly, n):
-        return poly[n] if n < len(poly) else jnp.zeros_like(largest)
-
+    step = np.array([1.0 / centre, 0.0, 0.0, 0.0, 0.0])
+    rest = np.array([1.0, 0.0, 0.0, 0.0, 0.0])
+    total = np.zeros(5)
     for k in range(4):
-        total = [total[n] + entry(step, n) for n in range(4)]
-        rest = [entry(rest, n) - (step[n - 1] if n > 0 else 0.0) for n in range(k + 2)]
+        total = total + step
+        rest = rest - np.concatenate([[0.0], step[:4]])
         if k < 3:
             new = 1.0 / (2.0 * spread - weight)
-            step = [
-                new * weight * entry(step, n) + 2.0 * new / radius * rest[n] for n in range(k + 2)
-            ]
+            step = new * weight * step + 2.0 * new / radius * rest
             weight = new
-    return total, rest
+    inverse = 1.0 / largest
+    powers = [None, inverse]
+    for n in range(2, 5):
+        powers.append(powers[-1] * inverse)
+    rests = [float(rest[n]) * (powers[n] if n else jnp.ones_like(largest)) for n in range(5)]
+    return [float(total[n]) * powers[n + 1] for n in range(4)], rests
 
 
 def kernel(
@@ -185,7 +181,7 @@
     send_x, send_y, send_e, got_x, got_y, got_e,
     rest, coarse_out, tails, tail_in, reach_in, elem_z, elem_out, elem_in, elem_c, vertex, gather,
     sums, norms, got_z, got_w,
-    send_sem, recv_sem, z_send, z_recv, w_send, w_recv, ez_send, ez_recv, cz_send, cz_recv,
+    send_sem, recv_sem, sum_send, sum_recv, ez_send, ez_recv, cz_send, cz_recv,
     er_send, er_recv, cr_send, cr_recv, in_sem, greeting,
 ):
     wide, cross = lax.axis_index("wide"), lax.axis_index("cross")
@@ -402,6 +398,8 @@
                 more = jnp.where(use, pltpu.roll(got_e[s, n - 4, c * 8 : c * 8 + 8], 64, 1), 0.0)
                 at = pl.ds(c * PER + j * 40 + i, 5, stride=8)
                 held[t, at] = held[t, at] + more[:5]
+
+    def exchange_sent(s):
         for n in range(8):
             @pl.when(present(n))
             def _(n=n):
@@ -494,27 +492,17 @@
         total = jnp.where(sub < 4, total, 0.0)
         return jnp.sum(total, axis=0, keepdims=True)
 
-    def z_sums():
-        return [
-            z_copy(sums.at[0, 0:1], got_z.at[k - 1 : k], z_send, z_recv, k)
-            for k in range(1, n_cross)
-        ]
-
-    def w_sums(slot):
-        return [
+    def start_sums(slot, peers, got, order):
+        for k in order:
             pltpu.make_async_remote_copy(
-                src_ref=sums.at[slot, 0:1], dst_ref=got_w.at[slot - 1, k : k + 1],
-                send_sem=w_send.at[slot - 1, k], recv_sem=w_recv.at[slot - 1, k],
-                device_id=w_peers[k], device_id_type=MESH)
-            for k in FAR_FIRST
-        ]
-
-    def finish_sums(copies, own, got):
-        for copy in copies:
-            copy.wait_recv()
-        total = own + jnp.sum(got[...], axis=0, keepdims=True)
-        for copy in copies:
-            copy.wait_send()
+                src_ref=sums.at[slot, 0:1], dst_ref=got.at[k : k + 1], send_sem=sum_send.at[slot],
+                recv_sem=sum_recv.at[slot], device_id=peers[k], device_id_type=MESH).start()
+
+    def finish_sums(slot, peers, got):
+        rows = got.at[0 : len(peers)]
+        pltpu.make_async_copy(rows, rows, sum_recv.at[slot]).wait()
+        total = sums[slot, 0:1] + jnp.sum(got[...], axis=0, keepdims=True)
+        pltpu.make_async_copy(rows, rows, sum_send.at[slot]).wait()
         return total
 
     def in_one_row(parts):
@@ -545,60 +533,10 @@
                                 greeting.at[stage, 1 - side], inc=1, device_id=(wide + by, cross),
                                 device_id_type=MESH)
 
-    def apply_all(base, squares, late=None):
-        def step(t, carry):
-            elements(t, t + 1)
-            gather_local(t + 1)
-
-            @pl.when(t == 0)
-            def _():
-                held[1] = load[...] - held[1]
-
-            s = lax.rem(t + base, 2)
-            exchange_start(t + 1, s)
-            if squares:
-                greet(t)
-                norms[pl.ds(t, 1)] = square(t)
-            if late is not None:
-                @pl.when(t == 3)
-                def _():
-                    late()
-            exchange_finish(t + 1, s)
-            return carry
-
-        lax.fori_loop(0, 4, step, 0)
-
-    exchange_start(0, 0)
-    loads[5].wait()
-    unpack(rhs_ref, load)
-    exchange_finish(0, 0)
-    apply_all(1, True)
-    norms[4:5] = square(4)
-    sums[0, 0:1] = in_one_row(norms[1:9])
-    copies = z_sums()
-    for copy in copies:
-        copy.start()
-    for k in range(1, n_cross):
-        z_copy(elem_z.at[cross], elem_z.at[cross], ez_send, ez_recv, k).start()
-    greet(4)
-    elements(4, 5)
-    sums[1, 0:1] = finish_sums(copies, sums[0, 0:1], got_z)
-    copies = w_sums(1)
-    for copy in copies:
-        copy.start()
-    for k in range(1, n_cross):
-        z_copy(elem_z.at[from_z(k)], elem_z.at[from_z(k)], ez_send, ez_recv, k).wait_recv()
-    for q in range(4):
-        for m in range(4):
-            elem_out[m * 4 + q : m * 4 + q + 1] = elem_z[q, m : m + 1]
-    for k in range(1, n_cross):
-        z_copy(elem_z.at[cross], elem_z.at[cross], ez_send, ez_recv, k).wait_send()
-    each_reach(lambda m: reach_out(elem_out, elem_in, er_send, er_recv, m), lambda c: c.start())
-
     points = gll_points()[0]
     here = jnp.where(sub < 4, 1.0, 0.0)
 
-    def restrict(n, carry):
+    def restrict(n):
         last = n == 4
         own_k = jnp.where(ends | last, 1.0, 0.0)
         own_j = jnp.where(last, keep_y, 0.0)
@@ -624,11 +562,116 @@
                         row = j2 * 12 + i2 * 6 + c * 2 + k
                         rest[cross, n, row : row + 1] = jnp.sum(
                             value * columns[i2], axis=0, keepdims=True)
-        return carry
-
-    lax.fori_loop(0, 5, restrict, 0)
-    for k in range(1, n_cross):
-        z_copy(rest.at[cross], rest.at[cross], cz_send, cz_recv, k).start()
+        for k in range(1, n_cross):
+            z_copy(rest.at[cross, n], rest.at[cross, n], cz_send.at[n], cz_recv.at[n], k).start()
+
+    def far_out(n):
+        return lambda m: reach_out(
+            coarse_out.at[n, 0:25], reach_in.at[n], cr_send.at[n], cr_recv.at[n], m)
+
+    def far_back(n):
+        return lambda m: reach_back(
+            coarse_out.at[n, 0:25], reach_in.at[n], cr_send.at[n], cr_recv.at[n], m)
+
+    def hand_on(n):
+        for k in range(1, n_cross):
+            z_copy(
+                rest.at[from_z(k), n], rest.at[from_z(k), n], cz_send.at[n], cz_recv.at[n], k
+            ).wait_recv()
+        before = jnp.zeros((12, LANES), f32)
+        for q in range(4):
+            ahead = rest[q, n, 12:24]
+            swapped = pltpu.roll(jnp.where(spread_to(low, 12), ahead, before), 64, 1)
+            before = ahead
+            value = rest[q, n, 0:12] + swapped
+            moved = pltpu.roll(value, 1, 1)
+            for i2 in range(2):
+                for c in range(3):
+                    first, last = i2 * 6 + c * 2, i2 * 6 + c * 2 + 1
+                    row = i2 * 12 + q * 3 + c
+                    coarse_out[n, row : row + 1] = value[first : first + 1] + jnp.where(
+                        inner[:1], moved[last : last + 1], 0.0)
+                    tails[row : row + 1] = value[last : last + 1]
+        late = pltpu.roll(
+            jnp.where(spread_to(ends, 24), tails[...], 0.0), 1, 1, stride=1, stride_axis=0)
+        coarse_out[n, 24:25] = jnp.sum(late, axis=0, keepdims=True)
+        each_reach(far_out(n), lambda c: c.start())
+        for k in range(1, n_cross):
+            z_copy(
+                rest.at[cross, n], rest.at[cross, n], cz_send.at[n], cz_recv.at[n], k).wait_send()
+
+    def elements_out():
+        for k in range(1, n_cross):
+            z_copy(elem_z.at[cross], elem_z.at[cross], ez_send, ez_recv, k).start()
+
+    def elements_on():
+        for k in range(1, n_cross):
+            z_copy(elem_z.at[from_z(k)], elem_z.at[from_z(k)], ez_send, ez_recv, k).wait_recv()
+        for q in range(4):
+            for m in range(4):
+                elem_out[m * 4 + q : m * 4 + q + 1] = elem_z[q, m : m + 1]
+        each_reach(
+            lambda m: reach_out(elem_out, elem_in, er_send, er_recv, m), lambda c: c.start())
+        for k in range(1, n_cross):
+            z_copy(elem_z.at[cross], elem_z.at[cross], ez_send, ez_recv, k).wait_send()
+
+    def apply_all(base, squares, late=None):
+        def step(t, carry):
+            elements(t, t + 1)
+            gather_local(t + 1)
+
+            @pl.when(t == 0)
+            def _():
+                held[1] = load[...] - held[1]
+
+            s = lax.rem(t + base, 2)
+            exchange_start(t + 1, s)
+            exchange_sent(1 - s)
+            if squares:
+                greet(t)
+                norms[pl.ds(t, 1)] = square(t)
+
+                @pl.when(t >= 1)
+                def _():
+                    restrict(t - 1)
+
+                @pl.when(t == 1)
+                def _():
+                    elements_out()
+
+                @pl.when(t >= 2)
+                def _():
+                    hand_on(t - 2)
+
+                @pl.when(t == 3)
+                def _():
+                    elements_on()
+            if late is not None:
+                @pl.when(t == 3)
+                def _():
+                    late()
+            exchange_finish(t + 1, s)
+            return carry
+
+        lax.fori_loop(0, 4, step, 0)
+
+    exchange_start(0, 0)
+    loads[5].wait()
+    unpack(rhs_ref, load)
+    exchange_finish(0, 0)
+    apply_all(1, True)
+    norms[4:5] = square(4)
+    sums[0, 0:1] = in_one_row(norms[1:9])
+    start_sums(0, z_peers, got_z, range(3))
+    elements(4, 5)
+    restrict(4)
+    greet(4)
+    restrict(3)
+    hand_on(2)
+    sums[1, 0:1] = finish_sums(0, z_peers, got_z)
+    start_sums(1, w_peers, got_w.at[0], FAR_FIRST)
+    hand_on(4)
+    hand_on(3)
 
     each_reach(lambda m: reach_back(elem_out, elem_in, er_send, er_recv, m), lambda c: c.wait_recv())
     for m, by in enumerate(REACH):
@@ -640,54 +683,21 @@
         elem_c[at : at + 8] = jnp.where(sub < 7, elem_c[at : at + 8], 0.0)
     each_reach(lambda m: reach_out(elem_out, elem_in, er_send, er_recv, m), lambda c: c.wait_send())
 
-    largest = estimate(out_of_row(finish_sums(copies, sums[1, 0:1], got_w.at[0])))
+    for n in (0, 1, 2, 3, 4):
+        each_reach(far_back(n), lambda c: c.wait_recv())
+    largest = estimate(out_of_row(finish_sums(1, w_peers, got_w.at[0])))
     step_poly, rest_poly = smoothing(largest, FINE_RATIO)
 
-    for k in range(1, n_cross):
-        z_copy(rest.at[from_z(k)], rest.at[from_z(k)], cz_send, cz_recv, k).wait_recv()
-    blocks = []
-    for q in range(4):
-        value = rest_poly[0] * rest[q, 0]
-        for n in range(1, 5):
-            value = value + rest_poly[n] * rest[q, n]
-        blocks.append(value)
-    for k in range(1, n_cross):
-        z_copy(rest.at[cross], rest.at[cross], cz_send, cz_recv, k).wait_send()
-    nothing = jnp.zeros((12, LANES), f32)
-    for q in range(4):
-        before = blocks[q - 1][12:24] if q > 0 else nothing
-        swapped = pltpu.roll(jnp.where(spread_to(low, 12), blocks[q][12:24], before), 64, 1)
-        value = blocks[q][0:12] + swapped
-        moved = pltpu.roll(value, 1, 1)
+    free = jnp.where(wide - HOME + sub < n_wide, 1.0, 0.0)
+    for by in (0,) + REACH:
+        part = None
+        for n in range(5):
+            source = coarse_out.at[n] if by == 0 else reach_in.at[n, REACH.index(by)]
+            term = rest_poly[n] * source[0:25]
+            part = term if part is None else part + term
         for i2 in range(2):
-            for c in range(3):
-                first, last = i2 * 6 + c * 2, i2 * 6 + c * 2 + 1
-                row = i2 * 12 + q * 3 + c
-                coarse_out[row : row + 1] = value[first : first + 1] + jnp.where(
-                    inner[:1], moved[last : last + 1], 0.0)
-                tails[row : row + 1] = value[last : last + 1]
-    late = pltpu.roll(
-        jnp.where(spread_to(ends, 24), tails[...], 0.0), 1, 1, stride=1, stride_axis=0)
-    coarse_out[24:25] = jnp.sum(late, axis=0, keepdims=True)
-    each_reach(lambda m: reach_out(coarse_out, reach_in, cr_send, cr_recv, m), lambda c: c.start())
-
-    def add_steps(c, carry):
-        at = pl.ds(pl.multiple_of(c * PER, 8), PER)
-        value = held[0, at]
-        for n in range(4):
-            value = value + step_poly[n] * held[n + 1, at]
-        held[0, at] = value
-        return carry
-
-    lax.fori_loop(0, 3, add_steps, 0)
-    each_reach(lambda m: reach_back(coarse_out, reach_in, cr_send, cr_recv, m), lambda c: c.wait_recv())
-
-    free = jnp.where(wide - HOME + sub < n_wide, 1.0, 0.0)
-    for i2 in range(2):
-        for by in (0,) + REACH:
             s = HOME + by + i2
             if 0 <= s < 8:
-                part = coarse_out if by == 0 else reach_in.at[REACH.index(by)]
                 gather[pl.ds(i2 * 96 + s, 12, stride=8)] = part[i2 * 12 : i2 * 12 + 12]
                 tail_in[i2 * 8 + s : i2 * 8 + s + 1] = part[24:25]
     for m in range(12):
@@ -696,7 +706,6 @@
         vertex[0, m * 16 : m * 16 + 8] = first * free
         vertex[0, m * 16 + 8 : m * 16 + 16] = free * jnp.where(
             outer, pltpu.roll(first, 127, 1), last)
-    each_reach(lambda m: reach_out(coarse_out, reach_in, cr_send, cr_recv, m), lambda c: c.wait_send())
 
     def close(n, q):
         for c in range(3):
@@ -797,10 +806,19 @@
     for n in range(4):
         norms[n : n + 1] = coarse_square(n)
     sums[2, 0:1] = in_one_row(norms[0:8])
-    copies = w_sums(2)
-    for copy in copies:
-        copy.start()
-    coarse_largest = estimate(out_of_row(finish_sums(copies, sums[2, 0:1], got_w.at[1])))
+    start_sums(2, w_peers, got_w.at[1], FAR_FIRST)
+    for n in range(5):
+        each_reach(far_out(n), lambda c: c.wait_send())
+    def add_steps(c, carry):
+        at = pl.ds(pl.multiple_of(c * PER, 8), PER)
+        value = held[0, at]
+        for n in range(4):
+            value = value + step_poly[n] * held[n + 1, at]
+        held[0, at] = value
+        return carry
+
+    lax.fori_loop(0, 3, add_steps, 0)
+    coarse_largest = estimate(out_of_row(finish_sums(2, w_peers, got_w.at[1])))
     coarse_poly, _ = smoothing(coarse_largest, COARSE_RATIO)
     left, right = column_ref[80:88], column_ref[88:96]
     for c in range(3):
@@ -862,6 +880,7 @@
 
     apply_all(1, False, lambda: to_nodes(most, out_ref))
     to_nodes(lambda at: step_poly[3] * held[4, at], last_ref)
+    exchange_sent(0)
 
 
 def on_device(rhs, start, stiffness, fibre_index):
@@ -906,10 +925,10 @@
             room(2, 2, FACE_Y, LANES),
             room(2, 4, EDGE, LANES),
             room(4, 5, 24, LANES),
-            room(32, LANES),
+            room(5, 32, LANES),
             room(24, LANES),
             room(16, LANES),
-            room(8, 32, LANES),
+            room(5, 8, 25, LANES),
             room(4, 8, LANES),
             room(16, LANES),
             room(8, 16, LANES),
@@ -922,11 +941,10 @@
             room(2, 32, LANES),
             flags(2, 8), flags(2, 8),
             flags(3), flags(3),
-            flags(2, 31), flags(2, 31),
             flags(3), flags(3),
-            flags(3), flags(3),
+            flags(5, 3), flags(5, 3),
             flags(8), flags(8),
-            flags(8), flags(8),
+            flags(5, 8), flags(5, 8),
             flags(6),
             pltpu.SemaphoreType.REGULAR((4, 2)),
         ],

time: 74.3 us -> 71.5 us (0.962); the launches traced: 74.2 us -> 70.6 us
  Pallas kernels: 71.3 us -> 67.7 us
    pallas_call x1, Pallas kernels: 71.3 us -> 67.7 us  [on_device(): pl.pallas_call(kernel, out_shape=(jax.ShapeDtypeStruct(rhs.shape, f32), j...]
where the time goes in v4:
time: 71.5 us; the launch traced here: 70.6 us
  Pallas kernels  67.7 us (95%)
  other arithmetic  1.66 us (2%)
    pallas_call x1, Pallas kernels, on_device(): pl.pallas_call(kernel, out_shape=(jax.ShapeDtypeStruct(rhs.shape, f32), j...  67.7 us
    add x1, other arithmetic, on_device(): return (most + last, correction)  1.66 us

profile of v4, /device:TPU:7, one launch (start us, length us, event | category | flops | bytes accessed | tf_op | source)
XLA Modules:
  0.0 70.6 jit_solution(4729194257711782671)
XLA Ops:
  0.6 67.7 %shard_map.77 = (f32[3,4,8,257]{3,2,1,0:T(8,128)}, f32[3,4,8,257]{3,2,1,0:T(8,128)}, f32[3,1,2,65]{3,2,1,0:T(2,128)}) custom-call(f32[3,4,8,257]{3,2,1,0:T(8,128)} %start_hbm.1, f32[3,4,8,257]{3,2,1,0:T(8,128)} %rhs_hbm.1, f32[1,2,64]{2,1,0:T(2,128)} %stiff_hbm.1, s32[1,2,64]{2,1,0:T(2,128)} %index_hbm.1, f32[200,128]{1,0:T(8,128)} %constant.4.clone.weight_hbm, ...), custom_call_target="tpu_custom_call" | custom-call | tf_op jit(solution)/shard_map/pallas_call | solution.py:897
  68.4 0.0 copy-start
  68.4 1.7 %add.3 = f32[3,4,8,257]{3,2,1,0:T(8,128)} add(f32[3,4,8,257]{3,2,1,0:T(8,128)} %get-tuple-element.5, f32[3,4,8,257]{3,2,1,0:T(8,128)} %get-tuple-element.6) | non-fusion elementwise | flops 24672 | bytes 296064 | tf_op jit(solution)/shard_map/add | solution.py:955
  70.0 0.0 copy-done
  70.0 0.6 copy.9
Async XLA Ops:
  68.4 1.7 %copy-start = (f32[3,1,2,65]{3,2,1,0:T(2,128)S(1)}, f32[3,1,2,65]{3,2,1,0:T(2,128)}, u32[]{:S(2)}) copy-start(f32[3,1,2,65]{3,2,1,0:T(2,128)} %get-tuple-element.11) | copy-start | bytes 4684

commit v5 on v4

--- a/solution.py
+++ b/solution.py
@@ -451,7 +451,7 @@
                         pull[k] + mass + across(flux_x, base + (c * PER + k * 8), 1))
             return carry
 
-        lax.fori_loop(0, 5, layer, 0)
+        lax.fori_loop(0, 5, layer, 0, unroll=True)
         for c in range(3):
             for k in range(5):
                 at = [c * PER + j * 40 + k * 8 for j in range(5)]

time: 71.5 us -> 71.1 us (level)
  no operation moved by 1% of the time
where the time goes in v5:
time: 71.1 us; the launch traced here: 70.2 us
  Pallas kernels  67.3 us (95%)
  other arithmetic  1.66 us (2%)
    pallas_call x1, Pallas kernels, on_device(): pl.pallas_call(kernel, out_shape=(jax.ShapeDtypeStruct(rhs.shape, f32), j...  67.3 us
    add x1, other arithmetic, on_device(): return (most + last, correction)  1.66 us

profile of v5, /device:TPU:7, one launch (start us, length us, event | category | flops | bytes accessed | tf_op | source)
XLA Modules:
  0.0 70.2 jit_solution(4077336365030052126)
XLA Ops:
  0.6 67.3 %shard_map.77 = (f32[3,4,8,257]{3,2,1,0:T(8,128)}, f32[3,4,8,257]{3,2,1,0:T(8,128)}, f32[3,1,2,65]{3,2,1,0:T(2,128)}) custom-call(f32[3,4,8,257]{3,2,1,0:T(8,128)} %start_hbm.1, f32[3,4,8,257]{3,2,1,0:T(8,128)} %rhs_hbm.1, f32[1,2,64]{2,1,0:T(2,128)} %stiff_hbm.1, s32[1,2,64]{2,1,0:T(2,128)} %index_hbm.1, f32[200,128]{1,0:T(8,128)} %constant.4.clone.weight_hbm, ...), custom_call_target="tpu_custom_call" | custom-call | tf_op jit(solution)/shard_map/pallas_call | solution.py:897
  67.9 0.0 copy-start
  67.9 1.7 %add.3 = f32[3,4,8,257]{3,2,1,0:T(8,128)} add(f32[3,4,8,257]{3,2,1,0:T(8,128)} %get-tuple-element.5, f32[3,4,8,257]{3,2,1,0:T(8,128)} %get-tuple-element.6) | non-fusion elementwise | flops 24672 | bytes 296064 | tf_op jit(solution)/shard_map/add | solution.py:955
  69.6 0.0 copy-done
  69.6 0.6 copy.9
Async XLA Ops:
  67.9 1.7 %copy-start = (f32[3,1,2,65]{3,2,1,0:T(2,128)S(1)}, f32[3,1,2,65]{3,2,1,0:T(2,128)}, u32[]{:S(2)}) copy-start(f32[3,1,2,65]{3,2,1,0:T(2,128)} %get-tuple-element.11) | copy-start | bytes 4684
